TPU v7x, 128 devices: a whole 4x4x4 slice. The times are simulated.
128 devices in a mesh: seq: 32 (over y_lo, z, x), chan: 4 (over y_hi, core).
Axes of the slice: x: 4, y: 4 (y_hi: 2, y_lo: 2; y = y_hi * 2 + y_lo), z: 4, core: 2. Of those that a mesh axis runs over, the one named last changes fastest.
Arguments:
- queries: bfloat16 [32768, 512], P('seq', 'chan'), may hold values from -6 to 6
- keys: bfloat16 [32768, 512], P('seq', 'chan'), may hold values from -6 to 6
- values: bfloat16 [32768, 512], P('seq', 'chan'), may hold values from -6 to 6
- cotangent: bfloat16 [32768, 512], P('seq', 'chan'), may hold values from -6 to 6
- out_weight: bfloat16 [512, 512], P('chan'), may hold values from -0.375 to 0.375
- taps: float32 [32768, 512], P('seq', 'chan'), may hold values from -1 to 1, as said below
- skip_gain: float32 [512], P('chan'), may hold values from 0.5 to 1.5
Outputs:
- out: bfloat16 [32768, 512], P('seq', 'chan')
- query_grad: bfloat16 [32768, 512], P('seq', 'chan')
- key_grad: bfloat16 [32768, 512], P('seq', 'chan')
- value_grad: bfloat16 [32768, 512], P('seq', 'chan')
- weight_grad: float32 [512, 512], P('chan')
- taps_grad: float32 [32768, 512], P('seq', 'chan')
- skip_grad: float32 [512], P('chan')
Inputs may be any that keep to these rules, and one draw needn't show every extreme that they name: taps holds each channel's filter value at lags 0 to 32767.
All inputs are finite; a program needn't handle non-finite values.
Results may differ from a plain program's by a relative error of at most 0.0049.
Values may be sent and summed in bfloat16 or wider, within the bound.
A program may use at most 64 MiB of HBM per device.

v0:
```python
import math

import jax
import jax.numpy as jnp
from jax import lax
from jax.sharding import PartitionSpec as P

COLS = 256


HIGHEST = lax.Precision.HIGHEST


def angle_pair(first_ids, second_ids, period):
    product = first_ids[:, None] * second_ids[None, :] % period
    angles = product.astype(jnp.float32) * (2.0 * math.pi / period)
    return (jnp.cos(angles), jnp.sin(angles))


def along_cols(table, block):
    return jnp.einsum("kn,pnc->pkc", table, block, precision=HIGHEST)


def spectral_product(left, right, conjugate):
    left_real, left_imag = (left[0], left[1])
    if conjugate:
        left_imag = -left_imag
    return jnp.stack(
        [left_real * right[0] - left_imag * right[1], left_real * right[1] + left_imag * right[0]]
    )


def local(queries, keys, values, cotangent, out_weight, taps, skip_gain):
    seq_count = lax.axis_size("seq")
    seq_place = lax.axis_index("seq")
    seq_dev = queries.shape[0]
    window = seq_dev * seq_count
    padded_len = 2 * window
    col_total = COLS
    col_share = col_total // seq_count
    row_total = padded_len // col_total
    row_share = row_total // seq_count
    row_half = row_total // 2
    rows_local = seq_dev // col_total
    inv_scale = 1.0 / padded_len
    row_ids = jnp.arange(row_total, dtype=jnp.int32)
    half_ids = jnp.arange(row_half, dtype=jnp.int32)
    col_ids = jnp.arange(col_total, dtype=jnp.int32)
    cos_a, sin_a = angle_pair(row_ids, half_ids, row_total)
    cos_b, sin_b = angle_pair(col_ids, col_ids, col_total)
    cos_c, sin_c = angle_pair(half_ids, row_ids, row_total)
    my_cols = seq_place * col_share + jnp.arange(col_share, dtype=jnp.int32)
    fwd_cos, fwd_sin = angle_pair(row_ids, my_cols, padded_len)
    my_rows = seq_place * row_share + jnp.arange(row_share, dtype=jnp.int32)
    inv_cos, inv_sin = angle_pair(my_rows, col_ids, padded_len)

    def forward_transform(signal):
        blocks = signal.reshape(rows_local, col_total, signal.shape[1])
        flat_rows = lax.all_to_all(blocks, "seq", split_axis=1, concat_axis=0, tiled=True).reshape(
            row_half, -1
        )
        real_part = jnp.dot(cos_a, flat_rows, precision=HIGHEST).reshape(row_total, col_share, -1)
        imag_part = -jnp.dot(sin_a, flat_rows, precision=HIGHEST).reshape(row_total, col_share, -1)
        twist_cos = fwd_cos[:, :, None]
        twist_sin = fwd_sin[:, :, None]
        spread = jnp.stack(
            [
                real_part * twist_cos + imag_part * twist_sin,
                imag_part * twist_cos - real_part * twist_sin,
            ]
        )
        segment = lax.all_to_all(spread, "seq", split_axis=1, concat_axis=2, tiled=True)
        real_part = segment[0]
        imag_part = segment[1]
        return jnp.stack(
            [
                along_cols(cos_b, real_part) + along_cols(sin_b, imag_part),
                along_cols(cos_b, imag_part) - along_cols(sin_b, real_part),
            ]
        )

    def inverse_transform(spectrum):
        real_part, imag_part = (spectrum[0], spectrum[1])
        back_real = along_cols(cos_b, real_part) - along_cols(sin_b, imag_part)
        back_imag = along_cols(cos_b, imag_part) + along_cols(sin_b, real_part)
        twist_cos = inv_cos[:, :, None]
        twist_sin = inv_sin[:, :, None]
        turned = jnp.stack(
            [
                back_real * twist_cos - back_imag * twist_sin,
                back_real * twist_sin + back_imag * twist_cos,
            ]
        )
        segment = lax.all_to_all(turned, "seq", split_axis=2, concat_axis=1, tiled=True)
        flat_real = segment[0].reshape(row_total, -1)
        flat_imag = segment[1].reshape(row_total, -1)
        first_out = (
            jnp.dot(cos_c, flat_real, precision=HIGHEST)
            - jnp.dot(sin_c, flat_imag, precision=HIGHEST)
        ) * inv_scale
        shaped = first_out.reshape(row_half, col_share, -1)
        gathered = shaped[None]
        restored = lax.all_to_all(gathered, "seq", split_axis=1, concat_axis=2, tiled=True)
        return restored.reshape(restored.shape[0], seq_dev, restored.shape[3])

    keys_f = keys.astype(jnp.float32)
    values_f = values.astype(jnp.float32)
    queries_f = queries.astype(jnp.float32)
    inner = keys_f * values_f
    inner_spec = forward_transform(inner)
    taps_spec = forward_transform(taps)
    conv = inverse_transform(spectral_product(taps_spec, inner_spec, False))[0]
    mixed = conv + skip_gain[None, :] * inner
    gated = (queries_f * mixed).astype(jnp.bfloat16)
    partial_out = jnp.dot(gated, out_weight, preferred_element_type=jnp.float32)
    out = lax.psum_scatter(partial_out, "chan", scatter_dimension=1, tiled=True).astype(
        jnp.bfloat16
    )
    segment = lax.all_gather(cotangent, "chan", axis=1, tiled=True)
    back_sum = lax.dot_general(
        segment, out_weight, (((1,), (1,)), ((), ())), preferred_element_type=jnp.float32
    )
    weight_term = lax.dot_general(
        gated, segment, (((0,), (0,)), ((), ())), preferred_element_type=jnp.float32
    )
    weight_total = lax.psum(weight_term, "seq")
    inner_cot = back_sum * queries_f
    query_grad = (back_sum * mixed).astype(jnp.bfloat16)
    cot_spec = forward_transform(inner_cot)
    first_spec = spectral_product(taps_spec, cot_spec, True)
    second_spec = spectral_product(inner_spec, cot_spec, True)
    back_conv = inverse_transform(first_spec)[0]
    taps_grad = inverse_transform(second_spec)[0]
    inner_grad = back_conv + skip_gain[None, :] * inner_cot
    key_grad = (inner_grad * values_f).astype(jnp.bfloat16)
    value_grad = (inner_grad * keys_f).astype(jnp.bfloat16)
    skip_part = jnp.sum(inner_cot * inner, axis=0)
    skip_total = lax.psum(skip_part, "seq")
    scale = 1.0 / math.sqrt(window)
    return (
        out,
        query_grad,
        key_grad,
        value_grad,
        weight_total * scale,
        taps_grad * scale,
        skip_total * scale,
    )


def solution(mesh):
    placed = (
        P("seq", "chan"),
        P("seq", "chan"),
        P("seq", "chan"),
        P("seq", "chan"),
        P("chan", None),
        P("seq", "chan"),
        P("chan"),
    )
    return jax.shard_map(
        local,
        mesh=mesh,
        in_specs=placed,
        out_specs=(
            P("seq", "chan"),
            P("seq", "chan"),
            P("seq", "chan"),
            P("seq", "chan"),
            P("chan", None),
            P("seq", "chan"),
            P("chan"),
        ),
        check_vma=False,
    )
```

profile of v0, /device:TPU:0, one launch (start us, length us, event | category | flops | bytes accessed | tf_op | source)
XLA Modules:
  0.0 693.8 jit_solution(15307604192312807470)
XLA Ops:
  8.0 2.2 copy.133
  10.2 9.3 %all-to-all-start = ((f32[4,256,128]{2,0,1:T(4,128)}), f32[4,256,128]{2,0,1:T(4,128)S(1)}, u32[]{:S(2)}, u32[]{:S(2)}) async-start(f32[4,256,128]{2,0,1:T(4,128)} %copy.133), calls=%async_computation | async-start | bytes 1048576 | tf_op jit(solution)/shard_map/all_to_all | solution.py:59
  19.4 17.2 %all-gather.2.cloned.1.call-done = bf16[1024,512]{1,0:T(8,128)(2,1)} async-done(((bf16[1024,128]{1,0:T(8,128)(2,1)}), bf16[1024,512]{1,0:T(8,128)(2,1)}) %all-gather.2.cloned.1.call-update) | async-done | bytes 1048592 | tf_op jit(solution)/shard_map/all_gather | solution.py:119
  36.7 2.5 multiply_reduce_fusion
  41.1 6.5 all-to-all-start.6
  50.8 8.6 %all-to-all-done.6 = f32[4,256,128]{2,0,1:T(4,128)S(1)} async-done(((f32[4,256,128]{2,0,1:T(4,128)}), f32[4,256,128]{2,0,1:T(4,128)S(1)}, u32[]{:S(2)}, u32[]{:S(2)}) %all-to-all-start.6) | async-done | bytes 524320 | tf_op jit(solution)/shard_map/all_to_all | solution.py:59
  59.4 4.8 all-to-all-start.2
  66.1 2.5 fusion.105
  68.6 6.1 all-to-all-done.2
  81.0 3.8 add_bitcast_fusion.2
  84.9 2.6 copy.137
  87.5 4.4 all-to-all-start.1
  93.3 2.6 copy.147
  95.9 22.3 %all-to-all-done.1 = f32[2,256,8,128]{3,2,0,1:T(8,128)S(1)} async-done(((f32[2,256,8,128]{3,2,0,1:T(8,128)}), f32[2,256,8,128]{3,2,0,1:T(8,128)S(1)}, u32[]{:S(2)}, u32[]{:S(2)}) %all-to-all-start.1) | async-done | bytes 2097184 | tf_op jit(solution)/shard_map/all_to_all | solution.py:72
  118.2 5.2 all-to-all-start.3
  124.9 2.6 copy.167
  127.8 3.7 fusion.43
  131.5 19.8 %all-to-all-done.3 = f32[2,256,8,128]{3,2,0,1:T(8,128)} async-done(((f32[2,256,8,128]{3,2,0,1:T(8,128)}), f32[2,256,8,128]{3,2,0,1:T(8,128)}, u32[]{:S(2)}, u32[]{:S(2)}) %all-to-all-start.3) | async-done | bytes 2097184 | tf_op jit(solution)/shard_map/all_to_all | solution.py:72
  151.3 5.0 all-to-all-start.7
  158.1 2.6 fusion.39
  161.0 2.6 fusion.33
  163.6 3.6 fusion.37
  167.2 3.6 fusion.5
  170.8 2.8 fusion.3
  173.6 2.7 fusion.2
  176.3 7.9 %all-to-all-done.7 = f32[2,256,8,128]{3,2,0,1:T(8,128)} async-done(((f32[2,256,8,128]{3,2,0,1:T(8,128)}), f32[2,256,8,128]{3,2,0,1:T(8,128)}, u32[]{:S(2)}, u32[]{:S(2)}) %all-to-all-start.7) | async-done | bytes 2097184 | tf_op jit(solution)/shard_map/all_to_all | solution.py:72
  186.1 2.7 fusion.31
  188.8 2.7 fusion.27
  191.5 2.9 fusion.1
  194.4 2.6 fusion.4
  197.1 3.3 multiply_subtract_fusion
  200.3 2.0 fusion.85
  202.3 2.0 fusion.87
  204.3 2.4 convolution_add_fusion.3
  206.7 2.0 fusion.81
  208.7 2.0 fusion.79
  210.7 2.0 convolution_subtract_fusion.1
  212.7 2.0 convolution_add_fusion.1
  214.7 2.0 fusion.77
  216.7 2.1 fusion.75
  218.8 2.0 convolution_subtract_fusion
  220.8 2.0 convolution_add_fusion
  222.8 4.5 subtract_bitcast_fusion
  227.4 2.0 copy.175
  229.4 4.8 all-to-all-start.8
  234.1 3.1 pad_maximum_fusion.2
  237.2 3.0 copy.157
  240.3 21.8 %all-to-all-done.8 = f32[2,8,256,128]{3,1,0,2:T(8,128)S(1)} async-done(((f32[2,8,256,128]{3,1,0,2:T(8,128)}), f32[2,8,256,128]{3,1,0,2:T(8,128)S(1)}, u32[]{:S(2)}, u32[]{:S(2)}) %all-to-all-start.8) | async-done | bytes 2097184 | tf_op jit(solution)/shard_map/all_to_all | solution.py:94
  263.4 5.0 all-to-all-start.4
  268.4 2.3 copy.301
  274.6 21.9 %all-to-all-done.4 = f32[2,8,256,128]{3,1,0,2:T(8,128)S(1)} async-done(((f32[2,8,256,128]{3,1,0,2:T(8,128)}), f32[2,8,256,128]{3,1,0,2:T(8,128)S(1)}, u32[]{:S(2)}, u32[]{:S(2)}) %all-to-all-start.4) | async-done | bytes 2097184 | tf_op jit(solution)/shard_map/all_to_all | solution.py:94
  296.4 5.1 all-to-all-start.9
  306.1 5.8 all-to-all-done.9
  312.0 4.6 all-to-all-start.5
  318.0 2.0 copy.181
  321.1 5.5 all-to-all-done.5
  326.6 4.3 all-to-all-start.10
  332.1 2.5 multiply_convert_fusion
  337.7 18.4 %all-to-all-done.10 = f32[2,8,256,128]{3,1,0,2:T(8,128)S(1)} async-done(((f32[2,8,256,128]{3,1,0,2:T(8,128)}), f32[2,8,256,128]{3,1,0,2:T(8,128)S(1)}, u32[]{:S(2)}, u32[]{:S(2)}) %all-to-all-start.10) | async-done | bytes 2097184 | tf_op jit(solution)/shard_map/all_to_all | solution.py:94
  360.7 4.5 all-to-all-start.11
  365.2 83.0 %psum.15 = f32[128]{0:T(128)S(1)} all-reduce(f32[128]{0:T(128)S(1)} %get-tuple-element.7), channel_id=1, replica_groups=mesh['seq'=32,'chan'=4] {'seq'}, use_global_device_ids=true, to_apply=%region_3.4 | all-reduce | flops 128 | bytes 1024 | tf_op jit(solution)/shard_map/psum | solution.py:138
  449.6 194.2 %all-reduce.2.cloned.1.call-done = f32[128,512]{1,0:T(8,128)} async-done(((f32[128,512]{1,0:T(8,128)}), f32[128,512]{1,0:T(8,128)}) %all-reduce.2.cloned.1.call-update) | async-done | bytes 262160 | tf_op jit(solution)/shard_map/psum | solution.py:126
  645.5 39.7 %reduce-scatter.2.cloned.1.call-done = f32[1024,128]{1,0:T(8,128)} async-done(((f32[1024,512]{1,0:T(8,128)}), f32[1024,128]{1,0:T(8,128)}) %reduce-scatter.2.cloned.1.call-update) | async-done | bytes 524304 | tf_op jit(solution)/shard_map/reduce_scatter | solution.py:116
  685.2 1.8 convert_element_type.128
  (98 shorter events, 45.5 us)
Async XLA Ops:
  7.2 29.5 %copy-start = (bf16[128,512]{1,0:T(8,128)(2,1)S(1)}, bf16[128,512]{1,0:T(8,128)(2,1)}, u32[]{:S(2)}) copy-start(bf16[128,512]{1,0:T(8,128)(2,1)} %param.11) | copy-start | bytes 393220
  7.2 29.5 %copy-start.13 = (bf16[1024,128]{1,0:T(8,128)(2,1)S(1)}, bf16[1024,128]{1,0:T(8,128)(2,1)}, u32[]{:S(2)}) copy-start(bf16[1024,128]{1,0:T(8,128)(2,1)} %param.7) | copy-start | bytes 786436
  7.2 29.5 %copy-start.12 = (bf16[1024,128]{1,0:T(8,128)(2,1)S(1)}, bf16[1024,128]{1,0:T(8,128)(2,1)}, u32[]{:S(2)}) copy-start(bf16[1024,128]{1,0:T(8,128)(2,1)} %param.8) | copy-start | bytes 786436
  7.2 29.5 %copy-start.11 = (bf16[1024,128]{1,0:T(8,128)(2,1)S(1)}, bf16[1024,128]{1,0:T(8,128)(2,1)}, u32[]{:S(2)}) copy-start(bf16[1024,128]{1,0:T(8,128)(2,1)} %param.9) | copy-start | bytes 786436
  7.2 29.4 %all-gather.2.cloned.1.call-start = ((), (), s32[]{:S(2)}) async-start(), calls=%async_computation.14 | async-start | bytes 1310720 | tf_op jit(solution)/shard_map/all_gather | solution.py:119
  10.2 31.0 %all-to-all-start = ((f32[4,256,128]{2,0,1:T(4,128)}), f32[4,256,128]{2,0,1:T(4,128)S(1)}, u32[]{:S(2)}, u32[]{:S(2)}) async-start(f32[4,256,128]{2,0,1:T(4,128)} %copy.133), calls=%async_computation | async-start | bytes 1048576 | tf_op jit(solution)/shard_map/all_to_all | solution.py:59
  39.1 0.8 copy-start.2
  41.1 18.3 %all-to-all-start.6 = ((f32[4,256,128]{2,0,1:T(4,128)}), f32[4,256,128]{2,0,1:T(4,128)S(1)}, u32[]{:S(2)}, u32[]{:S(2)}) async-start(f32[4,256,128]{2,0,1:T(4,128)} %copy.163), calls=%async_computation.7 | async-start | bytes 1048576 | tf_op jit(solution)/shard_map/all_to_all | solution.py:59
  59.4 15.3 %all-to-all-start.2 = ((f32[4,256,128]{2,0,1:T(4,128)}), f32[4,256,128]{2,0,1:T(4,128)}, u32[]{:S(2)}, u32[]{:S(2)}) async-start(f32[4,256,128]{2,0,1:T(4,128)} %copy.143), calls=%async_computation.2 | async-start | bytes 1048576 | tf_op jit(solution)/shard_map/all_to_all | solution.py:59
  78.0 2.9 copy-start.4
  87.5 4.5 copy-start.8
  87.5 30.7 %all-to-all-start.1 = ((f32[2,256,8,128]{3,2,0,1:T(8,128)}), f32[2,256,8,128]{3,2,0,1:T(8,128)S(1)}, u32[]{:S(2)}, u32[]{:S(2)}) async-start(f32[2,256,8,128]{3,2,0,1:T(8,128)} %copy.137), calls=%async_computation.1 | async-start | bytes 4194304 | tf_op jit(solution)/shard_map/all_to_all | solution.py:72
  95.9 27.6 %copy-start.7 = (f32[1,256,8,128]{3,1,2,0:T(8,128)S(1)}, f32[1,256,8,128]{3,1,2,0:T(8,128)}, u32[]{:S(2)}) copy-start(f32[1,256,8,128]{3,1,2,0:T(8,128)} %get-tuple-element.19) | copy-start | bytes 3145732
  118.2 33.1 %all-to-all-start.3 = ((f32[2,256,8,128]{3,2,0,1:T(8,128)}), f32[2,256,8,128]{3,2,0,1:T(8,128)}, u32[]{:S(2)}, u32[]{:S(2)}) async-start(f32[2,256,8,128]{3,2,0,1:T(8,128)} %copy.147), calls=%async_computation.3 | async-start | bytes 4194304 | tf_op jit(solution)/shard_map/all_to_all | solution.py:72
  151.3 32.9 %all-to-all-start.7 = ((f32[2,256,8,128]{3,2,0,1:T(8,128)}), f32[2,256,8,128]{3,2,0,1:T(8,128)}, u32[]{:S(2)}, u32[]{:S(2)}) async-start(f32[2,256,8,128]{3,2,0,1:T(8,128)} %copy.167), calls=%async_computation.8 | async-start | bytes 4194304 | tf_op jit(solution)/shard_map/all_to_all | solution.py:72
  160.9 6.3 copy-start.6
  191.5 2.9 copy-start.5
  194.4 2.7 copy-start.10
  229.4 32.7 %all-to-all-start.8 = ((f32[2,8,256,128]{3,1,0,2:T(8,128)}), f32[2,8,256,128]{3,1,0,2:T(8,128)S(1)}, u32[]{:S(2)}, u32[]{:S(2)}) async-start(f32[2,8,256,128]{3,1,0,2:T(8,128)} %copy.175), calls=%async_computation.9 | async-start | bytes 4194304 | tf_op jit(solution)/shard_map/all_to_all | solution.py:94
  262.1 1.3 copy-start.1
  263.4 33.0 %all-to-all-start.4 = ((f32[2,8,256,128]{3,1,0,2:T(8,128)}), f32[2,8,256,128]{3,1,0,2:T(8,128)S(1)}, u32[]{:S(2)}, u32[]{:S(2)}) async-start(f32[2,8,256,128]{3,1,0,2:T(8,128)} %copy.157), calls=%async_computation.4 | async-start | bytes 4194304 | tf_op jit(solution)/shard_map/all_to_all | solution.py:94
  296.4 15.5 %all-to-all-start.9 = ((f32[1,128,8,128]{3,2,0,1:T(8,128)}), f32[1,128,8,128]{3,2,0,1:T(8,128)}, u32[]{:S(2)}, u32[]{:S(2)}) async-start(f32[1,128,8,128]{3,2,0,1:T(8,128)} %bitcast_bitcast_fusion.1), calls=%async_computation.10 | async-start | bytes 1048576 | tf_op jit(solution)/shard_map/all_to_all | solution.py:103
  312.0 14.6 %all-to-all-start.5 = ((f32[1,128,8,128]{3,2,0,1:T(8,128)}), f32[1,128,8,128]{3,2,0,1:T(8,128)}, u32[]{:S(2)}, u32[]{:S(2)}) async-start(f32[1,128,8,128]{3,2,0,1:T(8,128)} %bitcast_bitcast_fusion.3), calls=%async_computation.5 | async-start | bytes 1048576 | tf_op jit(solution)/shard_map/all_to_all | solution.py:103
  321.1 11.0 %copy-start.3 = (f32[1024,128]{1,0:T(8,128)S(1)}, f32[1024,128]{1,0:T(8,128)}, u32[]{:S(2)}) copy-start(f32[1024,128]{1,0:T(8,128)} %copy-done.2) | copy-start | bytes 1572868
  321.1 11.0 %copy-start.14 = (f32[128]{0:T(128)S(1)}, f32[128]{0:T(128)}, u32[]{:S(2)}) copy-start(f32[128]{0:T(128)} %param.13) | copy-start | bytes 1540
  326.6 29.5 %all-to-all-start.10 = ((f32[2,8,256,128]{3,1,0,2:T(8,128)}), f32[2,8,256,128]{3,1,0,2:T(8,128)S(1)}, u32[]{:S(2)}, u32[]{:S(2)}) async-start(f32[2,8,256,128]{3,1,0,2:T(8,128)} %copy.181), calls=%async_computation.11 | async-start | bytes 4194304 | tf_op jit(solution)/shard_map/all_to_all | solution.py:94
  330.9 312.9 %all-reduce.2.cloned.1.call-start = ((), (), s32[]{:S(2)}) async-start(), calls=%async_computation.15 | async-start | bytes 524288 | tf_op jit(solution)/shard_map/psum | solution.py:126
  332.0 2.6 copy-start.9
  335.7 349.6 %reduce-scatter.2.cloned.1.call-start = ((), (), s32[]{:S(2)}) async-start(), calls=%async_computation.13 | async-start | bytes 2621440 | tf_op jit(solution)/shard_map/reduce_scatter | solution.py:116
  360.7 88.0 %all-to-all-start.11 = ((f32[1,128,8,128]{3,2,0,1:T(8,128)}), f32[1,128,8,128]{3,2,0,1:T(8,128)S(1)}, u32[]{:S(2)}, u32[]{:S(2)}) async-start(f32[1,128,8,128]{3,2,0,1:T(8,128)} %bitcast_bitcast_fusion), calls=%async_computation.12 | async-start | bytes 1048576 | tf_op jit(solution)/shard_map/all_to_all | solution.py:103
Sparse Core Ops, SparseCore 0:
  9.7 26.8 all-gather.1
  335.8 307.9 all-reduce.1
  646.6 38.5 reduce-scatter.1
where the time goes:
time: 700 us; the launch traced here: 694 us
  waiting for transfers between devices  390 us (56%)
  matrix products  87.4 us (12%)
  blocking collectives  83 us (12%)
  starting transfers between devices  63.8 us (9%)
  local copies, waits for them, and re-layouts  40.5 us (6%)
  between operations  14.8 us (2%)
  other arithmetic  14.3 us (2%)
    psum x1, waiting for transfers between devices, local(): weight_total = lax.psum(weight_term, 'seq')  194 us
    psum x1, blocking collectives, local(): skip_total = lax.psum(skip_part, 'seq')  83 us
    dot_general x24, matrix products, along_cols(): return jnp.einsum('kn,pnc->pkc', table, block, precision=HIGHEST)  62.5 us
    all_to_all x3, waiting for transfers between devices, inverse_transform(): lax.all_to_all(turned, 'seq', split_axis=2, concat_axis=1, tiled=True)  62 us
    all_to_all x3, waiting for transfers between devices, forward_transform(): lax.all_to_all(spread, 'seq', split_axis=1, concat_axis=2, tiled=True)  50.1 us
    reduce_scatter x1, waiting for transfers between devices, local(): lax.psum_scatter(partial_out, 'chan', scatter_dimension=1, tiled=True)  39.7 us
    all_to_all x3, starting transfers between devices, forward_transform(): lax.all_to_all(blocks, 'seq', split_axis=1, concat_axis=0, tiled=True)  20.5 us
    all_gather x1, waiting for transfers between devices, local(): segment = lax.all_gather(cotangent, 'chan', axis=1, tiled=True)  17.2 us
  transfers between devices with their start and end apart: 15, of which 13 were waited for; matrix products, arithmetic and copies ran while one was open for 12% of the time, Pallas kernels for 0%

commit v1 on v0

v1 whole, which is shorter than its diff:
```python
import functools
import math

import jax
import jax.numpy as jnp
import numpy as np
from jax import lax
from jax.experimental import pallas as pl
from jax.experimental.pallas import tpu as pltpu
from jax.sharding import PartitionSpec as P

MESH = pl.DeviceIdType.MESH
BF16 = jnp.bfloat16
F32 = jnp.float32
LANES = 128
CHUNKS = 4


def split_table(table):
    high = table.astype(BF16)
    low = (table - high.astype(np.float64)).astype(BF16)
    return jnp.asarray(np.stack([high, low]))


def tables(rows):
    count = rows * LANES
    ids = np.arange(rows)
    lane = np.arange(LANES)
    first = 2.0 * np.pi * (((4 * ids[:, None] + 1) * ids[None, :]) % (4 * rows)) / (4 * rows)
    second = 2.0 * np.pi * ((lane[:, None] * lane[None, :]) % LANES) / LANES
    twist = 2.0 * np.pi * ((4 * ids[:, None] + 1) * lane[None, :]) / (4 * count)
    cos, sin = np.cos(second), np.sin(second)
    return (
        split_table(np.concatenate([np.cos(first), np.sin(first)], axis=0)),
        split_table(np.block([[cos, sin], [-sin, cos]])),
        split_table(np.block([[cos, -sin], [sin, cos]])),
        split_table(np.concatenate([np.cos(first).T, np.sin(first).T], axis=1) / count),
        jnp.asarray(np.stack([np.cos(twist), np.sin(twist)]), F32),
    )


def dot(left, right):
    return jnp.dot(left, right, preferred_element_type=F32)


def split(value):
    high = value.astype(BF16)
    return high, (value - high.astype(F32)).astype(BF16)


def kernel(
    n,
    keys,
    values,
    queries,
    taps,
    cot,
    weight,
    gain,
    fa_in,
    fb_in,
    gb_in,
    ga_in,
    tw_in,
    out_o,
    query_o,
    key_o,
    value_o,
    weight_o,
    taps_o,
    skip_o,
    fa,
    fb,
    gb,
    ga,
    tw,
    stage,
    first_send,
    first_recv,
    cot_send,
    cot_recv,
    conv_send,
    conv_recv,
    grad_send,
    grad_recv,
    weight_send,
    weight_recv,
    total_send,
    total_recv,
    cot_all,
    gated_all,
    columns,
    back,
    inner_cot,
    xb,
    t_high,
    t_low,
    d_high,
    d_low,
    spec_inner,
    spec_taps,
    spec_cot,
    table_sem,
    send_sem,
    recv_sem,
    chan_send,
    chan_recv,
    relay_send,
    relay_recv,
    col_send,
    col_recv,
):
    me = lax.axis_index("seq")
    lane = lax.axis_index("chan")
    core, chip = lax.rem(lane, 2), lane // 2
    twin = 2 * chip + 1 - core
    mirror = 2 * (1 - chip) + core
    corner = 2 * (1 - chip) + 1 - core
    positions = keys.shape[0]
    blocks = positions // LANES
    rows = n * blocks
    own = LANES // n
    piece = own * blocks
    window = positions * n
    scale = 1.0 / math.sqrt(window)

    barrier = pltpu.get_barrier_semaphore()

    def greet(step, carry):
        pl.semaphore_signal(
            barrier, inc=1, device_id={"seq": lax.rem(me + step, n)}, device_id_type=MESH
        )
        return carry

    for partner in (mirror, twin, corner):
        pl.semaphore_signal(barrier, inc=1, device_id={"chan": partner}, device_id_type=MESH)
    lax.fori_loop(1, n, greet, 0)

    copies = [
        pltpu.make_async_copy(src, dst, table_sem.at[i])
        for i, (src, dst) in enumerate(
            ((fa_in, fa), (fb_in, fb), (gb_in, gb), (ga_in, ga), (tw_in, tw))
        )
    ]
    for copy in copies:
        copy.start()

    def exchange(src, dst, phase, source=None):
        def step(offset, carry):
            peer = lax.rem(me + offset, n)
            pltpu.make_async_remote_copy(
                src_ref=src.at[peer] if source is None else source,
                dst_ref=dst.at[me],
                send_sem=send_sem.at[phase],
                recv_sem=recv_sem.at[phase],
                device_id={"seq": peer},
                device_id_type=MESH,
            ).start()
            return carry

        lax.fori_loop(1, n, step, 0)
        dst[me] = src[me] if source is None else source[...]

    def await_all(buf, sem):
        part = buf.at[pl.ds(0, n - 1)]
        pltpu.make_async_copy(part, part, sem).wait()

    def pack(value, dst, index):
        for b in range(blocks):
            stage[pl.ds(b, LANES, stride=blocks), :] = value(b).T
        dst[:, index] = stage[...].astype(BF16).reshape(n, piece, LANES)

    def unpack(src, index):
        stage[...] = src[:, index].astype(F32).reshape(n * piece, LANES)
        return lambda b: stage[pl.ds(b, LANES, stride=blocks), :].T

    def block(ref, b):
        return ref[b * LANES : (b + 1) * LANES, :].astype(F32)

    def gather(src, buf, phase):
        size = positions // CHUNKS
        started = []
        for k in range(CHUNKS):
            part = pl.ds(k * size, size)
            started.append(
                pltpu.make_async_remote_copy(
                    src_ref=src.at[part],
                    dst_ref=buf.at[lane, part],
                    send_sem=chan_send.at[phase, 0, k],
                    recv_sem=chan_recv.at[phase, 0, k],
                    device_id={"chan": mirror},
                    device_id_type=MESH,
                )
            )
            started[-1].start()
        near = pltpu.make_async_remote_copy(
            src_ref=src,
            dst_ref=buf.at[lane],
            send_sem=chan_send.at[phase, 1, 0],
            recv_sem=chan_recv.at[phase, 1, 0],
            device_id={"chan": twin},
            device_id_type=MESH,
        )
        near.start()
        return started, near

    def relay(buf, phase, started):
        size = positions // CHUNKS
        passed = []
        for k in range(CHUNKS):
            part = pl.ds(k * size, size)
            started[k].wait_recv()
            passed.append(
                pltpu.make_async_remote_copy(
                    src_ref=buf.at[mirror, part],
                    dst_ref=buf.at[mirror, part],
                    send_sem=relay_send.at[phase, k],
                    recv_sem=relay_recv.at[phase, k],
                    device_id={"chan": twin},
                    device_id_type=MESH,
                )
            )
            passed[-1].start()
        return passed

    pack(lambda b: block(keys, b) * block(values, b), first_send, 0)
    pl.semaphore_wait(barrier, n + 2)
    cot_started, cot_near = gather(cot, cot_all, 0)
    col_copies = []
    for k, partner in enumerate((mirror, twin, corner)):
        col_copies.append(
            pltpu.make_async_remote_copy(
                src_ref=weight.at[:, pl.ds(pl.multiple_of(partner * LANES, LANES), LANES)],
                dst_ref=columns.at[lane],
                send_sem=col_send.at[k],
                recv_sem=col_recv.at[k],
                device_id={"chan": partner},
                device_id_type=MESH,
            )
        )
        col_copies[-1].start()
    pack(lambda b: block(taps, b), first_send, 1)
    exchange(first_send, first_recv, 0)
    cot_all[lane] = cot[...]
    columns[lane] = weight[:, pl.ds(pl.multiple_of(lane * LANES, LANES), LANES)]

    cot_passed = relay(cot_all, 0, cot_started)
    cot_near.wait_recv()
    for copy in cot_passed:
        copy.wait_recv()
    for b in range(blocks):
        part = pl.ds(b * LANES, LANES)
        total = jnp.zeros((LANES, LANES), F32)
        for g in range(0, 4, 2):
            left = jnp.concatenate([cot_all[g, part], cot_all[g + 1, part]], axis=1)
            total += lax.dot_general(
                left,
                weight[:, g * LANES : (g + 2) * LANES],
                (((1,), (1,)), ((), ())),
                preferred_element_type=F32,
            )
        back[part, :] = total
        inner_cot[part, :] = total * block(queries, b)
    pack(lambda b: inner_cot[b * LANES : (b + 1) * LANES, :], cot_send, 0)
    exchange(cot_send, cot_recv, 1)

    def forward(src, index, spec):
        for pair in range(own // 2):
            x = src[:, index, 16 * pair : 16 * pair + 16, :].astype(F32)
            for half in range(2):
                xb[:, (2 * pair + half) * LANES : (2 * pair + half + 1) * LANES] = (
                    x[:, 8 * half : 8 * half + 8, :].reshape(rows, LANES).astype(BF16)
                )
        for pair in range(own // 2):
            cols = xb[:, 2 * pair * LANES : (2 * pair + 2) * LANES]
            a = dot(fa[0], cols) + dot(fa[1], cols)
            for half in range(2):
                real = a[:rows, half * LANES : (half + 1) * LANES]
                imag = a[rows:, half * LANES : (half + 1) * LANES]
                c = 2 * pair + half
                t = jnp.concatenate(
                    [real * tw[0] - imag * tw[1], real * tw[1] + imag * tw[0]], axis=1
                )
                t_high[c * rows : (c + 1) * rows, :], t_low[c * rows : (c + 1) * rows, :] = split(t)
        for c in range(own):
            part = slice(c * rows, (c + 1) * rows)
            spec[part, :] = (
                dot(t_high[part, :], fb[0]) + dot(t_high[part, :], fb[1]) + dot(t_low[part, :], fb[0])
            )

    def inverse(left, right, conjugate, dst, index):
        sign = -1.0 if conjugate else 1.0
        for c in range(own):
            part = slice(c * rows, (c + 1) * rows)
            l_real, l_imag = left[part, :LANES], sign * left[part, LANES:]
            r_real, r_imag = right[part, :LANES], right[part, LANES:]
            high, low = split(
                jnp.concatenate(
                    [l_real * r_real - l_imag * r_imag, l_real * r_imag + l_imag * r_real], axis=1
                )
            )
            y = dot(high, gb[0]) + dot(high, gb[1]) + dot(low, gb[0])
            real, imag = y[:, :LANES], y[:, LANES:]
            d_real = split(real * tw[0] + imag * tw[1])
            d_imag = split(imag * tw[0] - real * tw[1])
            cols = slice(c * LANES, (c + 1) * LANES)
            d_high[:rows, cols], d_low[:rows, cols] = d_real
            d_high[rows:, cols], d_low[rows:, cols] = d_imag
        for pair in range(own // 2):
            cols = slice(2 * pair * LANES, (2 * pair + 2) * LANES)
            y = dot(ga[0], d_high[:, cols]) + dot(ga[1], d_high[:, cols]) + dot(ga[0], d_low[:, cols])
            dst[:, index, 16 * pair : 16 * pair + 16, :] = jnp.concatenate(
                [y[:, :LANES].reshape(n, 8, LANES), y[:, LANES:].reshape(n, 8, LANES)], axis=1
            ).astype(BF16)

    for copy in copies:
        copy.wait()
    await_all(first_recv, recv_sem.at[0])
    forward(first_recv, 0, spec_inner)
    forward(first_recv, 1, spec_taps)
    inverse(spec_taps, spec_inner, False, conv_send, 0)
    exchange(conv_send, conv_recv, 2)

    await_all(cot_recv, recv_sem.at[1])
    forward(cot_recv, 0, spec_cot)
    inverse(spec_taps, spec_cot, True, grad_send, 0)
    inverse(spec_inner, spec_cot, True, grad_send, 1)
    exchange(grad_send, grad_recv, 3)

    await_all(conv_recv, recv_sem.at[2])
    conv = unpack(conv_recv, 0)
    skip = jnp.zeros((8, LANES), F32)
    for b in range(blocks):
        part = pl.ds(b * LANES, LANES)
        inner = block(keys, b) * block(values, b)
        mixed = conv(b) + gain[...] * inner
        gated_all[lane, part, :] = (block(queries, b) * mixed).astype(BF16)
        query_o[part, :] = (back[part, :] * mixed).astype(BF16)
        skip += jnp.sum((inner_cot[part, :] * inner).reshape(LANES // 8, 8, LANES), axis=0)
    gated_started, gated_near = gather(gated_all.at[lane], gated_all, 1)
    skip_high, skip_low = split(skip)
    tail = jnp.concatenate([skip_high.astype(F32), skip_low.astype(F32)], axis=0).astype(BF16)
    gated = gated_all[lane]
    share = 4 * LANES // n
    for g in range(4):
        term = lax.dot_general(
            gated, cot_all[g], (((0,), (0,)), ((), ())), preferred_element_type=F32
        ).astype(BF16)
        count = LANES // share
        weight_send[g * count : (g + 1) * count, :share, :] = term.reshape(count, share, LANES)
    weight_send[:, share:, :] = jnp.broadcast_to(tail[None], (n, 16, LANES))
    exchange(weight_send, weight_recv, 4)
    gated_passed = relay(gated_all, 1, gated_started)

    await_all(weight_recv, recv_sem.at[4])
    sums = jnp.sum(weight_recv[...].astype(F32), axis=0)
    total_send[...] = sums[:share] * scale
    exchange(None, total_recv, 5, source=total_send)
    skip_o[...] = jnp.sum(sums[share:], axis=0, keepdims=True) * scale

    await_all(grad_recv, recv_sem.at[3])
    grad = unpack(grad_recv, 0)
    for b in range(blocks):
        part = pl.ds(b * LANES, LANES)
        inner_grad = grad(b) + gain[...] * inner_cot[part, :]
        key_o[part, :] = (inner_grad * block(values, b)).astype(BF16)
        value_o[part, :] = (inner_grad * block(keys, b)).astype(BF16)
    grad = unpack(grad_recv, 1)
    for b in range(blocks):
        taps_o[pl.ds(b * LANES, LANES), :] = grad(b) * scale

    gated_near.wait_recv()
    for copy in gated_passed:
        copy.wait_recv()
    for copy in col_copies:
        copy.wait_recv()
    half = positions // 2
    for k in range(2):
        part = pl.ds(k * half, half)
        total = jnp.zeros((half, LANES), F32)
        for g in range(0, 4, 2):
            left = jnp.concatenate([gated_all[g, part], gated_all[g + 1, part]], axis=1)
            total += dot(left, columns[g : g + 2].reshape(2 * LANES, LANES))
        out_o[part, :] = total.astype(BF16)

    await_all(total_recv, recv_sem.at[5])
    for g in range(4):
        count = LANES // share
        weight_o[:, g * LANES : (g + 1) * LANES] = total_recv[
            g * count : (g + 1) * count
        ].reshape(LANES, LANES)

    for buf, phase in (
        (first_send, 0),
        (cot_send, 1),
        (conv_send, 2),
        (grad_send, 3),
        (weight_send, 4),
        (total_recv, 5),
    ):
        await_all(buf, send_sem.at[phase])
    for copy in cot_started + gated_started + cot_passed + gated_passed + col_copies:
        copy.wait_send()
    cot_near.wait_send()
    gated_near.wait_send()


def local(n, queries, keys, values, cotangent, out_weight, taps, skip_gain):
    positions = keys.shape[0]
    blocks = positions // LANES
    rows = n * blocks
    own = LANES // n
    piece = own * blocks
    share = 4 * LANES // n
    vmem = pl.BlockSpec(memory_space=pltpu.VMEM)
    anywhere = pl.BlockSpec(memory_space=pl.ANY)
    wide = jax.ShapeDtypeStruct((positions, LANES), BF16)

    def buffers(count):
        return [pltpu.VMEM((n, count, piece, LANES), BF16)] * 2

    outs = pl.pallas_call(
        functools.partial(kernel, n),
        out_shape=[
            wide,
            wide,
            wide,
            wide,
            jax.ShapeDtypeStruct((LANES, 4 * LANES), F32),
            jax.ShapeDtypeStruct((positions, LANES), F32),
            jax.ShapeDtypeStruct((1, LANES), F32),
        ],
        in_specs=[vmem] * 7 + [anywhere] * 5,
        out_specs=[vmem] * 7,
        scratch_shapes=[
            pltpu.VMEM((2, 2 * rows, rows), BF16),
            pltpu.VMEM((2, 2 * LANES, 2 * LANES), BF16),
            pltpu.VMEM((2, 2 * LANES, 2 * LANES), BF16),
            pltpu.VMEM((2, rows, 2 * rows), BF16),
            pltpu.VMEM((2, rows, LANES), F32),
            pltpu.VMEM((positions, LANES), F32),
            *buffers(2),
            *buffers(1),
            *buffers(1),
            *buffers(2),
            pltpu.VMEM((n, share + 16, LANES), BF16),
            pltpu.VMEM((n, share + 16, LANES), BF16),
            pltpu.VMEM((share, LANES), F32),
            pltpu.VMEM((n, share, LANES), F32),
            pltpu.VMEM((4, positions, LANES), BF16),
            pltpu.VMEM((4, positions, LANES), BF16),
            pltpu.VMEM((4, LANES, LANES), BF16),
            pltpu.VMEM((positions, LANES), F32),
            pltpu.VMEM((positions, LANES), F32),
            pltpu.VMEM((rows, own * LANES), BF16),
            pltpu.VMEM((own * rows, 2 * LANES), BF16),
            pltpu.VMEM((own * rows, 2 * LANES), BF16),
            pltpu.VMEM((2 * rows, own * LANES), BF16),
            pltpu.VMEM((2 * rows, own * LANES), BF16),
            pltpu.VMEM((own * rows, 2 * LANES), F32),
            pltpu.VMEM((own * rows, 2 * LANES), F32),
            pltpu.VMEM((own * rows, 2 * LANES), F32),
            pltpu.SemaphoreType.DMA((5,)),
            pltpu.SemaphoreType.DMA((6,)),
            pltpu.SemaphoreType.DMA((6,)),
            pltpu.SemaphoreType.DMA((2, 2, CHUNKS)),
            pltpu.SemaphoreType.DMA((2, 2, CHUNKS)),
            pltpu.SemaphoreType.DMA((2, CHUNKS)),
            pltpu.SemaphoreType.DMA((2, CHUNKS)),
            pltpu.SemaphoreType.DMA((3,)),
            pltpu.SemaphoreType.DMA((3,)),
        ],
        compiler_params=pltpu.CompilerParams(
            collective_id=0, has_side_effects=True, vmem_limit_bytes=48 * 1024 * 1024
        ),
        name="hyena",
    )(
        keys,
        values,
        queries,
        taps,
        cotangent,
        out_weight,
        skip_gain.reshape(1, LANES),
        *tables(rows),
    )
    return (*outs[:6], outs[6].reshape(LANES))


def solution(mesh):
    wide = P("seq", "chan")
    return jax.shard_map(
        functools.partial(local, mesh.shape["seq"]),
        mesh=mesh,
        in_specs=(wide, wide, wide, wide, P("chan", None), wide, P("chan")),
        out_specs=(wide, wide, wide, wide, P("chan", None), wide, P("chan")),
        check_vma=False,
    )
```

time: 700 us -> 74.4 us (0.11)
  waiting for transfers between devices: 390 us -> 0 us
  matrix products: 87.4 us -> 0 us
  blocking collectives: 83 us -> 0 us
  starting transfers between devices: 63.8 us -> 0 us
  Pallas kernels: 0 us -> 57.1 us
  local copies, waits for them, and re-layouts: 40.5 us -> 16.1 us
  other arithmetic: 14.3 us -> 0 us
  between operations: 14.8 us -> 0.67 us
    psum x1 -> x0, waiting for transfers between devices: 194 us -> none  [local(): weight_total = lax.psum(weight_term, 'seq')]
    all_to_all x12 -> x0, waiting for transfers between devices: 138 us -> none  [the longest x3 62 us: inverse_transform(): lax.all_to_all(turned, 'seq', split_axis=2, concat_axis=1, tiled=True)]
    dot_general x39 -> x0, matrix products: 87.4 us -> none  [the longest x24 62.5 us: along_cols(): return jnp.einsum('kn,pnc->pkc', table, block, precision=HIGHEST)]
    psum x1 -> x0, blocking collectives: 83 us -> none  [local(): skip_total = lax.psum(skip_part, 'seq')]
    all_to_all x12 -> x0, starting transfers between devices: 63.4 us -> none  [the longest x3 20.5 us: forward_transform(): lax.all_to_all(blocks, 'seq', split_axis=1, concat_axis=0, tiled=True)]
    pallas_call x0 -> x1, Pallas kernels: none -> 57.1 us  [local(): pl.pallas_call(functools.partial(kernel, n), out_shape=[wide, wide, wide,...]
    reduce_scatter x1 -> x0, waiting for transfers between devices: 39.7 us -> none  [local(): lax.psum_scatter(partial_out, 'chan', scatter_dimension=1, tiled=True)]
    all_gather x1 -> x0, waiting for transfers between devices: 17.2 us -> none  [local(): segment = lax.all_gather(cotangent, 'chan', axis=1, tiled=True)]
  transfers between devices with their start and end apart: 15 -> 0, of which waited for: 13 -> 0; matrix products, arithmetic and copies ran while one was open for 12% -> 0% of each run, Pallas kernels for 0% -> 0%
where the time goes in v1:
time: 74.4 us; the launch traced here: 73.9 us
  Pallas kernels  57.1 us (77%)
  local copies, waits for them, and re-layouts  16.1 us (22%)
    pallas_call x1, Pallas kernels, local(): pl.pallas_call(functools.partial(kernel, n), out_shape=[wide, wide, wide,...  57.1 us
    unnamed x31, local copies, waits for them, and re-layouts  16.1 us

profile of v1, /device:TPU:0, one launch (start us, length us, event | category | flops | bytes accessed | tf_op | source)
XLA Modules:
  0.0 73.9 jit_solution(10747749048904980940)
XLA Ops:
  0.6 0.0 copy-start.11
  0.6 0.6 copy-done.11
  1.3 0.0 copy-start
  1.3 1.0 %copy-done = f32[1024,128]{1,0:T(8,128)S(1)} copy-done((f32[1024,128]{1,0:T(8,128)S(1)}, f32[1024,128]{1,0:T(8,128)}, u32[]{:S(2)}) %copy-start) | copy-done | bytes 524312
  2.3 0.0 copy-start.1
  2.3 1.0 %copy-done.1 = bf16[2,256,512]{2,1,0:T(8,128)(2,1)S(1)} copy-done((bf16[2,256,512]{2,1,0:T(8,128)(2,1)S(1)}, bf16[2,256,512]{2,1,0:T(8,128)(2,1)}, u32[]{:S(2)}) %copy-start.1) | copy-done | bytes 524312
  3.4 0.0 copy-start.2
  3.4 1.0 %copy-done.2 = bf16[2,512,256]{2,1,0:T(8,128)(2,1)S(1)} copy-done((bf16[2,512,256]{2,1,0:T(8,128)(2,1)S(1)}, bf16[2,512,256]{2,1,0:T(8,128)(2,1)}, u32[]{:S(2)}) %copy-start.2) | copy-done | bytes 524312
  4.4 0.0 copy-start.3
  4.4 0.9 %copy-done.3 = bf16[1024,128]{1,0:T(8,128)(2,1)S(1)} copy-done((bf16[1024,128]{1,0:T(8,128)(2,1)S(1)}, bf16[1024,128]{1,0:T(8,128)(2,1)}, u32[]{:S(2)}) %copy-start.3) | copy-done | bytes 262168
  5.4 0.0 copy-start.4
  5.4 0.9 %copy-done.4 = bf16[1024,128]{1,0:T(8,128)(2,1)S(1)} copy-done((bf16[1024,128]{1,0:T(8,128)(2,1)S(1)}, bf16[1024,128]{1,0:T(8,128)(2,1)}, u32[]{:S(2)}) %copy-start.4) | copy-done | bytes 262168
  6.3 0.0 copy-start.5
  6.3 0.9 %copy-done.5 = bf16[1024,128]{1,0:T(8,128)(2,1)S(1)} copy-done((bf16[1024,128]{1,0:T(8,128)(2,1)S(1)}, bf16[1024,128]{1,0:T(8,128)(2,1)}, u32[]{:S(2)}) %copy-start.5) | copy-done | bytes 262168
  7.3 0.0 copy-start.6
  7.3 0.9 %copy-done.6 = bf16[1024,128]{1,0:T(8,128)(2,1)S(1)} copy-done((bf16[1024,128]{1,0:T(8,128)(2,1)S(1)}, bf16[1024,128]{1,0:T(8,128)(2,1)}, u32[]{:S(2)}) %copy-start.6) | copy-done | bytes 262168
  8.2 0.0 copy-start.7
  8.2 0.9 %copy-done.7 = f32[2,256,128]{2,1,0:T(8,128)S(1)} copy-done((f32[2,256,128]{2,1,0:T(8,128)S(1)}, f32[2,256,128]{2,1,0:T(8,128)}, u32[]{:S(2)}) %copy-start.7) | copy-done | bytes 262168
  9.2 0.0 copy-start.8
  9.2 0.9 %copy-done.8 = bf16[2,256,256]{2,1,0:T(8,128)(2,1)S(1)} copy-done((bf16[2,256,256]{2,1,0:T(8,128)(2,1)S(1)}, bf16[2,256,256]{2,1,0:T(8,128)(2,1)}, u32[]{:S(2)}) %copy-start.8) | copy-done | bytes 262168
  10.1 0.0 copy-start.9
  10.1 0.9 %copy-done.9 = bf16[2,256,256]{2,1,0:T(8,128)(2,1)S(1)} copy-done((bf16[2,256,256]{2,1,0:T(8,128)(2,1)S(1)}, bf16[2,256,256]{2,1,0:T(8,128)(2,1)}, u32[]{:S(2)}) %copy-start.9) | copy-done | bytes 262168
  11.1 0.0 copy-start.10
  11.1 0.9 %copy-done.10 = bf16[128,512]{1,0:T(8,128)(2,1)S(1)} copy-done((bf16[128,512]{1,0:T(8,128)(2,1)S(1)}, bf16[128,512]{1,0:T(8,128)(2,1)}, u32[]{:S(2)}) %copy-start.10) | copy-done | bytes 131096
  12.0 57.1 %hyena.1 = (bf16[1024,128]{1,0:T(8,128)(2,1)S(1)}, bf16[1024,128]{1,0:T(8,128)(2,1)S(1)}, bf16[1024,128]{1,0:T(8,128)(2,1)S(1)}, bf16[1024,128]{1,0:T(8,128)(2,1...) custom-call(bf16[1024,128]{1,0:T(8,128)(2,1)S(1)} %copy-done.3, ...), custom_call_target="tpu_custom_call" | custom-call | tf_op jit(solution)/shard_map/hyena/pallas_call | solution.py:422
  69.1 0.7 copy.26
  69.8 0.7 copy.27
  70.5 0.7 copy.28
  71.2 0.7 copy.29
  71.9 0.7 copy.30
  72.6 0.8 %copy.31 = f32[1024,128]{1,0:T(8,128)} copy(f32[1024,128]{1,0:T(8,128)S(1)} %get-tuple-element.33) | data formatting | bytes 1048576
  73.4 0.5 copy.32
Async XLA Ops:
  0.6 0.7 copy-start.11
  1.3 1.0 %copy-start = (f32[1024,128]{1,0:T(8,128)S(1)}, f32[1024,128]{1,0:T(8,128)}, u32[]{:S(2)}) copy-start(f32[1024,128]{1,0:T(8,128)} %taps.1) | copy-start | bytes 1572868
  2.3 1.0 %copy-start.1 = (bf16[2,256,512]{2,1,0:T(8,128)(2,1)S(1)}, bf16[2,256,512]{2,1,0:T(8,128)(2,1)}, u32[]{:S(2)}) copy-start(bf16[2,256,512]{2,1,0:T(8,128)(2,1)} %constant.13.clone.ga_in) | copy-start | bytes 1572868
  3.4 1.0 %copy-start.2 = (bf16[2,512,256]{2,1,0:T(8,128)(2,1)S(1)}, bf16[2,512,256]{2,1,0:T(8,128)(2,1)}, u32[]{:S(2)}) copy-start(bf16[2,512,256]{2,1,0:T(8,128)(2,1)} %constant.10.clone.fa_in) | copy-start | bytes 1572868
  4.4 0.9 %copy-start.3 = (bf16[1024,128]{1,0:T(8,128)(2,1)S(1)}, bf16[1024,128]{1,0:T(8,128)(2,1)}, u32[]{:S(2)}) copy-start(bf16[1024,128]{1,0:T(8,128)(2,1)} %keys.1) | copy-start | bytes 786436
  5.4 0.9 %copy-start.4 = (bf16[1024,128]{1,0:T(8,128)(2,1)S(1)}, bf16[1024,128]{1,0:T(8,128)(2,1)}, u32[]{:S(2)}) copy-start(bf16[1024,128]{1,0:T(8,128)(2,1)} %values.1) | copy-start | bytes 786436
  6.3 0.9 %copy-start.5 = (bf16[1024,128]{1,0:T(8,128)(2,1)S(1)}, bf16[1024,128]{1,0:T(8,128)(2,1)}, u32[]{:S(2)}) copy-start(bf16[1024,128]{1,0:T(8,128)(2,1)} %queries.1) | copy-start | bytes 786436
  7.3 0.9 %copy-start.6 = (bf16[1024,128]{1,0:T(8,128)(2,1)S(1)}, bf16[1024,128]{1,0:T(8,128)(2,1)}, u32[]{:S(2)}) copy-start(bf16[1024,128]{1,0:T(8,128)(2,1)} %cot.1) | copy-start | bytes 786436
  8.2 0.9 %copy-start.7 = (f32[2,256,128]{2,1,0:T(8,128)S(1)}, f32[2,256,128]{2,1,0:T(8,128)}, u32[]{:S(2)}) copy-start(f32[2,256,128]{2,1,0:T(8,128)} %constant.14.clone.tw_in) | copy-start | bytes 786436
  9.2 0.9 %copy-start.8 = (bf16[2,256,256]{2,1,0:T(8,128)(2,1)S(1)}, bf16[2,256,256]{2,1,0:T(8,128)(2,1)}, u32[]{:S(2)}) copy-start(bf16[2,256,256]{2,1,0:T(8,128)(2,1)} %constant.12.clone.gb_in) | copy-start | bytes 786436
  10.1 0.9 %copy-start.9 = (bf16[2,256,256]{2,1,0:T(8,128)(2,1)S(1)}, bf16[2,256,256]{2,1,0:T(8,128)(2,1)}, u32[]{:S(2)}) copy-start(bf16[2,256,256]{2,1,0:T(8,128)(2,1)} %constant.11.clone.fb_in) | copy-start | bytes 786436
  11.1 0.9 %copy-start.10 = (bf16[128,512]{1,0:T(8,128)(2,1)S(1)}, bf16[128,512]{1,0:T(8,128)(2,1)}, u32[]{:S(2)}) copy-start(bf16[128,512]{1,0:T(8,128)(2,1)} %weight.1) | copy-start | bytes 393220

commit v2 on v1

v2 whole, which is shorter than its diff:
```python
import functools
import math

import jax
import jax.numpy as jnp
import numpy as np
from jax import lax
from jax.experimental import pallas as pl
from jax.experimental.pallas import tpu as pltpu
from jax.sharding import PartitionSpec as P

MESH = pl.DeviceIdType.MESH
BF16 = jnp.bfloat16
F32 = jnp.float32
LANES = 128
CHUNKS = 4


def split_table(table):
    high = table.astype(BF16)
    low = (table - high.astype(np.float64)).astype(BF16)
    return jnp.asarray(np.stack([high, low]))


def tables(rows):
    count = rows * LANES
    ids = np.arange(rows)
    lane = np.arange(LANES)
    first = 2.0 * np.pi * (((4 * ids[:, None] + 1) * ids[None, :]) % (4 * rows)) / (4 * rows)
    second = 2.0 * np.pi * ((lane[:, None] * lane[None, :]) % LANES) / LANES
    twist = 2.0 * np.pi * ((4 * ids[:, None] + 1) * lane[None, :]) / (4 * count)
    cos, sin = np.cos(second), np.sin(second)
    return (
        split_table(np.concatenate([np.cos(first), np.sin(first)], axis=0)),
        jnp.asarray(np.stack([np.cos(twist), np.sin(twist)]), F32),
        split_table(np.block([[cos, sin], [-sin, cos]])),
        split_table(np.block([[cos, -sin], [sin, cos]])),
        split_table(np.concatenate([np.cos(first).T, np.sin(first).T], axis=1) / count),
    )


def in_hbm(array):
    return pltpu.with_memory_space_constraint(array, pltpu.HBM)


def dot(left, right):
    return jnp.dot(left, right, preferred_element_type=F32)


def split(value):
    high = value.astype(BF16)
    return high, (value - high.astype(F32)).astype(BF16)


def kernel(
    n,
    keys_in,
    values_in,
    taps_in,
    cot_in,
    weight_in,
    queries_in,
    fa_in,
    tw_in,
    fb_in,
    gb_in,
    ga_in,
    gain_in,
    out_o,
    query_o,
    weight_o,
    skip_o,
    inner_cot,
    grad_recv,
    keys,
    values,
    taps,
    cot_all,
    weight,
    queries,
    fa,
    tw,
    fb,
    gb,
    ga,
    gain,
    stage,
    first_send,
    first_recv,
    cot_send,
    cot_recv,
    conv_send,
    conv_recv,
    grad_send,
    weight_send,
    weight_recv,
    pair_send,
    pair_recv,
    total_recv,
    gated_all,
    columns,
    back,
    xb,
    t_high,
    t_low,
    d_high,
    d_low,
    spec_inner,
    spec_taps,
    spec_cot,
    table_sem,
    send_sem,
    recv_sem,
    chan_send,
    chan_recv,
    relay_send,
    relay_recv,
    col_send,
    col_recv,
):
    me = lax.axis_index("seq")
    lane = lax.axis_index("chan")
    core, chip = lax.rem(lane, 2), lane // 2
    twin = 2 * chip + 1 - core
    mirror = 2 * (1 - chip) + core
    corner = 2 * (1 - chip) + 1 - core
    positions = keys.shape[0]
    blocks = positions // LANES
    rows = n * blocks
    own = LANES // n
    piece = own * blocks
    window = positions * n
    scale = 1.0 / math.sqrt(window)

    barrier = pltpu.get_barrier_semaphore()

    def greet(step, carry):
        pl.semaphore_signal(
            barrier, inc=1, device_id={"seq": lax.rem(me + step, n)}, device_id_type=MESH
        )
        return carry

    for partner in (mirror, twin, corner):
        pl.semaphore_signal(barrier, inc=1, device_id={"chan": partner}, device_id_type=MESH)
    lax.fori_loop(1, n, greet, 0)

    pairs = (
        (keys_in, keys),
        (values_in, values),
        (taps_in, taps),
        (cot_in, cot_all.at[lane]),
        (weight_in, weight),
        (queries_in, queries),
        (fa_in, fa),
        (tw_in, tw),
        (fb_in, fb),
        (gb_in, gb),
        (ga_in, ga),
        (gain_in, gain),
    )
    copies = [
        pltpu.make_async_copy(src, dst, table_sem.at[i]) for i, (src, dst) in enumerate(pairs)
    ]
    for copy in copies:
        copy.start()

    plane = n // 2
    here, spot = me // plane, lax.rem(me, plane)
    across = 1 - here

    def send(src, dst, phase, peer):
        pltpu.make_async_remote_copy(
            src_ref=src,
            dst_ref=dst,
            send_sem=send_sem.at[phase],
            recv_sem=recv_sem.at[phase],
            device_id={"seq": peer},
            device_id_type=MESH,
        ).start()

    def exchange(src, dst, phase, half, index=None):
        def at(ref, slot):
            return ref.at[slot] if index is None else ref.at[slot, index]

        def step(offset, carry):
            peer = half * plane + lax.rem(spot + offset, plane)
            send(at(src, peer), at(dst, me), phase, peer)
            return carry

        lax.fori_loop(1 if half is here else 0, plane, step, 0)
        if half is here:
            if index is None:
                dst[me] = src[me]
            else:
                dst[me, index] = src[me, index]

    def exchange_all(src, dst, phase, index=None):
        exchange(src, dst, phase, across, index)
        exchange(src, dst, phase, here, index)

    def await_all(buf, sems, phase, count=n - 1, index=None):
        part = buf.at[pl.ds(0, count)] if index is None else buf.at[pl.ds(0, count), index]
        pltpu.make_async_copy(part, part, sems.at[phase]).wait()

    def pack(value, dst, index):
        for b in range(blocks):
            stage[pl.ds(b, LANES, stride=blocks), :] = value(b).T
        dst[:, index] = stage[...].astype(BF16).reshape(n, piece, LANES)

    def unpack(src, index):
        stage[...] = src[:, index].astype(F32).reshape(n * piece, LANES)
        return lambda b: stage[pl.ds(b, LANES, stride=blocks), :].T

    def block(ref, b):
        return ref[b * LANES : (b + 1) * LANES, :].astype(F32)

    def gather(src, buf, phase):
        size = positions // CHUNKS
        started = []
        for k in range(CHUNKS):
            part = pl.ds(k * size, size)
            started.append(
                pltpu.make_async_remote_copy(
                    src_ref=src.at[part],
                    dst_ref=buf.at[lane, part],
                    send_sem=chan_send.at[phase, 0, k],
                    recv_sem=chan_recv.at[phase, 0, k],
                    device_id={"chan": mirror},
                    device_id_type=MESH,
                )
            )
            started[-1].start()
        near = pltpu.make_async_remote_copy(
            src_ref=src,
            dst_ref=buf.at[lane],
            send_sem=chan_send.at[phase, 1, 0],
            recv_sem=chan_recv.at[phase, 1, 0],
            device_id={"chan": twin},
            device_id_type=MESH,
        )
        near.start()
        return started, near

    def relay(buf, phase, started):
        size = positions // CHUNKS
        passed = []
        for k in range(CHUNKS):
            part = pl.ds(k * size, size)
            started[k].wait_recv()
            passed.append(
                pltpu.make_async_remote_copy(
                    src_ref=buf.at[mirror, part],
                    dst_ref=buf.at[mirror, part],
                    send_sem=relay_send.at[phase, k],
                    recv_sem=relay_recv.at[phase, k],
                    device_id={"chan": twin},
                    device_id_type=MESH,
                )
            )
            passed[-1].start()
        return passed

    def forward(src, index, spec):
        for pair in range(own // 2):
            x = src[:, index, 16 * pair : 16 * pair + 16, :].astype(F32)
            for half in range(2):
                xb[:, (2 * pair + half) * LANES : (2 * pair + half + 1) * LANES] = (
                    x[:, 8 * half : 8 * half + 8, :].reshape(rows, LANES).astype(BF16)
                )
        for pair in range(own // 2):
            cols = xb[:, 2 * pair * LANES : (2 * pair + 2) * LANES]
            a = dot(fa[0], cols) + dot(fa[1], cols)
            for half in range(2):
                real = a[:rows, half * LANES : (half + 1) * LANES]
                imag = a[rows:, half * LANES : (half + 1) * LANES]
                c = 2 * pair + half
                t = jnp.concatenate(
                    [real * tw[0] - imag * tw[1], real * tw[1] + imag * tw[0]], axis=1
                )
                t_high[c * rows : (c + 1) * rows, :], t_low[c * rows : (c + 1) * rows, :] = split(t)
        for c in range(own):
            part = slice(c * rows, (c + 1) * rows)
            spec[part, :] = (
                dot(t_high[part, :], fb[0]) + dot(t_high[part, :], fb[1]) + dot(t_low[part, :], fb[0])
            )

    def inverse(left, right, conjugate, dst, index):
        sign = -1.0 if conjugate else 1.0
        for c in range(own):
            part = slice(c * rows, (c + 1) * rows)
            l_real, l_imag = left[part, :LANES], sign * left[part, LANES:]
            r_real, r_imag = right[part, :LANES], right[part, LANES:]
            high, low = split(
                jnp.concatenate(
                    [l_real * r_real - l_imag * r_imag, l_real * r_imag + l_imag * r_real], axis=1
                )
            )
            y = dot(high, gb[0]) + dot(high, gb[1]) + dot(low, gb[0])
            real, imag = y[:, :LANES], y[:, LANES:]
            d_real = split(real * tw[0] + imag * tw[1])
            d_imag = split(imag * tw[0] - real * tw[1])
            cols = slice(c * LANES, (c + 1) * LANES)
            d_high[:rows, cols], d_low[:rows, cols] = d_real
            d_high[rows:, cols], d_low[rows:, cols] = d_imag
        for pair in range(own // 2):
            cols = slice(2 * pair * LANES, (2 * pair + 2) * LANES)
            y = dot(ga[0], d_high[:, cols]) + dot(ga[1], d_high[:, cols]) + dot(ga[0], d_low[:, cols])
            dst[:, index, 16 * pair : 16 * pair + 16, :] = jnp.concatenate(
                [y[:, :LANES].reshape(n, 8, LANES), y[:, LANES:].reshape(n, 8, LANES)], axis=1
            ).astype(BF16)

    col_copies = [
        pltpu.make_async_remote_copy(
            src_ref=weight.at[:, pl.ds(pl.multiple_of(partner * LANES, LANES), LANES)],
            dst_ref=columns.at[lane],
            send_sem=col_send.at[k],
            recv_sem=col_recv.at[k],
            device_id={"chan": partner},
            device_id_type=MESH,
        )
        for k, partner in enumerate((mirror, twin, corner))
    ]
    share = 4 * LANES // plane
    count = LANES // share
    held = {}

    def first_out():
        exchange_all(first_send, first_recv, 0)

    def cot_out():
        held["cot"], held["cot_near"] = gather(cot_in, cot_all, 0)

    def cot_relay():
        for copy in copies[3:6]:
            copy.wait()
        held["cot_passed"] = relay(cot_all, 0, held["cot"])

    def columns_out():
        for copy in col_copies:
            copy.start()
        columns[lane] = weight[:, pl.ds(pl.multiple_of(lane * LANES, LANES), LANES)]

    def cot_signal():
        held["cot_near"].wait_recv()
        for copy in held["cot_passed"]:
            copy.wait_recv()
        for b in range(blocks):
            part = pl.ds(b * LANES, LANES)
            total = jnp.zeros((LANES, LANES), F32)
            for g in range(0, 4, 2):
                left = jnp.concatenate([cot_all[g, part], cot_all[g + 1, part]], axis=1)
                total += lax.dot_general(
                    left,
                    weight[:, g * LANES : (g + 2) * LANES],
                    (((1,), (1,)), ((), ())),
                    preferred_element_type=F32,
                )
            back[part, :] = total
            inner_cot[part, :] = total * block(queries, b)
        pack(lambda b: inner_cot[b * LANES : (b + 1) * LANES, :], cot_send, 0)
        exchange_all(cot_send, cot_recv, 1)

    def conv_signal():
        for copy in copies[6:]:
            copy.wait()
        await_all(first_recv, recv_sem, 0)
        forward(first_recv, 0, spec_inner)
        forward(first_recv, 1, spec_taps)
        inverse(spec_taps, spec_inner, False, conv_send, 0)
        exchange_all(conv_send, conv_recv, 2)

    def grad_signal():
        await_all(cot_recv, recv_sem, 1)
        forward(cot_recv, 0, spec_cot)
        inverse(spec_taps, spec_cot, True, grad_send, 0)
        exchange_all(grad_send, grad_recv, 3, 0)

    def taps_signal():
        inverse(spec_inner, spec_cot, True, grad_send, 1)
        exchange_all(grad_send, grad_recv, 4, 1)

    def gate():
        await_all(conv_recv, recv_sem, 2)
        conv = unpack(conv_recv, 0)
        skip = jnp.zeros((8, LANES), F32)
        for b in range(blocks):
            part = pl.ds(b * LANES, LANES)
            inner = block(keys, b) * block(values, b)
            mixed = conv(b) + gain[...] * inner
            gated_all[lane, part, :] = (block(queries, b) * mixed).astype(BF16)
            query_o[part, :] = (back[part, :] * mixed).astype(BF16)
            skip += jnp.sum((inner_cot[part, :] * inner).reshape(LANES // 8, 8, LANES), axis=0)
        held["gated"], held["gated_near"] = gather(gated_all.at[lane], gated_all, 1)
        held["skip"] = skip

    def weight_out():
        skip_high, skip_low = split(held["skip"])
        tail = jnp.concatenate([skip_high.astype(F32), skip_low.astype(F32)], axis=0).astype(BF16)
        gated = gated_all[lane]
        for g in range(4):
            term = lax.dot_general(
                gated, cot_all[g], (((0,), (0,)), ((), ())), preferred_element_type=F32
            ).astype(BF16)
            weight_send[g * count : (g + 1) * count, :share, :] = term.reshape(count, share, LANES)
        weight_send[:, share:, :] = jnp.broadcast_to(tail[None], (plane, 16, LANES))

        def spread(offset, carry):
            place = lax.rem(spot + offset, plane)
            send(weight_send.at[place], weight_recv.at[spot], 5, here * plane + place)
            return carry

        lax.fori_loop(1, plane, spread, 0)
        weight_recv[spot] = weight_send[spot]

    def weight_pair():
        await_all(weight_recv, recv_sem, 5, plane - 1)
        sums = jnp.sum(weight_recv[...].astype(F32), axis=0)
        pair_send[:share, :] = sums[:share]
        pair_send[share:, :] = sums[share : share + 8] + sums[share + 8 :]
        send(pair_send, pair_recv, 6, across * plane + spot)

    def weight_total():
        pltpu.make_async_copy(pair_recv, pair_recv, recv_sem.at[6]).wait()
        sums = (pair_send[...] + pair_recv[...]) * scale
        total_recv[spot] = sums[:share]
        skip_o[...] = jnp.sum(sums[share:], axis=0, keepdims=True)

        def collect(offset, carry):
            place = lax.rem(spot + offset, plane)
            send(total_recv.at[spot], total_recv.at[spot], 7, here * plane + place)
            return carry

        lax.fori_loop(1, plane, collect, 0)

    def gated_relay():
        held["gated_passed"] = relay(gated_all, 1, held["gated"])

    def project():
        held["gated_near"].wait_recv()
        for copy in held["gated_passed"] + col_copies:
            copy.wait_recv()
        half = positions // 2
        for k in range(2):
            part = pl.ds(k * half, half)
            total = jnp.zeros((half, LANES), F32)
            for g in range(0, 4, 2):
                left = jnp.concatenate([gated_all[g, part], gated_all[g + 1, part]], axis=1)
                total += dot(left, columns[g : g + 2].reshape(2 * LANES, LANES))
            out_o[part, :] = total.astype(BF16)

    def settle():
        await_all(total_recv, recv_sem, 7, plane - 1)
        for g in range(4):
            weight_o[:, g * LANES : (g + 1) * LANES] = total_recv[
                g * count : (g + 1) * count
            ].reshape(LANES, LANES)
        await_all(grad_recv, recv_sem, 3, index=0)
        await_all(grad_recv, recv_sem, 4, index=1)
        await_all(first_send, send_sem, 0)
        await_all(cot_send, send_sem, 1)
        await_all(conv_send, send_sem, 2)
        await_all(grad_send, send_sem, 3, index=0)
        await_all(grad_send, send_sem, 4, index=1)
        await_all(weight_send, send_sem, 5, plane - 1)
        pltpu.make_async_copy(pair_send, pair_send, send_sem.at[6]).wait()
        await_all(total_recv, send_sem, 7, plane - 1)
        for name in ("cot", "cot_passed", "gated", "gated_passed"):
            for copy in held[name]:
                copy.wait_send()
        for copy in col_copies + [held["cot_near"], held["gated_near"]]:
            copy.wait_send()

    copies[0].wait()
    copies[1].wait()
    pack(lambda b: block(keys, b) * block(values, b), first_send, 0)
    copies[2].wait()
    pack(lambda b: block(taps, b), first_send, 1)
    pl.semaphore_wait(barrier, n + 2)
    for step in (
        first_out,
        cot_out,
        conv_signal,
        cot_relay,
        cot_signal,
        columns_out,
        gate,
        weight_out,
        grad_signal,
        weight_pair,
        taps_signal,
        weight_total,
        gated_relay,
        project,
        settle,
    ):
        step()


def finish(
    n,
    keys_in,
    values_in,
    gain_in,
    out_i,
    query_i,
    weight_i,
    skip_i,
    inner_cot,
    grad_recv,
    out_o,
    query_o,
    key_o,
    value_o,
    weight_o,
    taps_o,
    skip_o,
    keys,
    values,
    gain,
    stage,
    key_v,
    value_v,
    taps_v,
    sem,
):
    positions = keys.shape[0]
    blocks = positions // LANES
    scale = 1.0 / math.sqrt(positions * n)
    loads = [
        pltpu.make_async_copy(src, dst, sem.at[i])
        for i, (src, dst) in enumerate(((keys_in, keys), (values_in, values), (gain_in, gain)))
    ]
    stores = [
        pltpu.make_async_copy(src, dst, sem.at[3 + i])
        for i, (src, dst) in enumerate(
            (
                (out_i, out_o),
                (query_i, query_o),
                (weight_i, weight_o),
                (skip_i, skip_o),
                (taps_v, taps_o),
                (key_v, key_o),
                (value_v, value_o),
            )
        )
    ]
    for copy in loads + stores[:4]:
        copy.start()

    def unpack(index):
        stage[...] = grad_recv[:, index].astype(F32).reshape(positions, LANES)
        return lambda b: stage[pl.ds(b, LANES, stride=blocks), :].T

    grad = unpack(1)
    for b in range(blocks):
        taps_v[pl.ds(b * LANES, LANES), :] = grad(b) * scale
    stores[4].start()
    for copy in loads:
        copy.wait()
    grad = unpack(0)
    for b in range(blocks):
        part = pl.ds(b * LANES, LANES)
        inner_grad = grad(b) + gain[...] * inner_cot[part, :]
        key_v[part, :] = (inner_grad * values[part, :].astype(F32)).astype(BF16)
        value_v[part, :] = (inner_grad * keys[part, :].astype(F32)).astype(BF16)
    stores[5].start()
    stores[6].start()
    for copy in stores:
        copy.wait()


def local(n, queries, keys, values, cotangent, out_weight, taps, skip_gain):
    positions = keys.shape[0]
    blocks = positions // LANES
    rows = n * blocks
    own = LANES // n
    piece = own * blocks
    plane = n // 2
    share = 4 * LANES // plane
    vmem = pl.BlockSpec(memory_space=pltpu.VMEM)
    far = pl.BlockSpec(memory_space=pltpu.HBM)
    wide = jax.ShapeDtypeStruct((positions, LANES), BF16)
    wide_f32 = jax.ShapeDtypeStruct((positions, LANES), F32)
    square = jax.ShapeDtypeStruct((LANES, 4 * LANES), F32)
    line = jax.ShapeDtypeStruct((1, LANES), F32)
    gain = skip_gain.reshape(1, LANES)

    def buffer(count):
        return pltpu.VMEM((n, count, piece, LANES), BF16)

    first = pl.pallas_call(
        functools.partial(kernel, n),
        out_shape=[
            wide,
            wide,
            square,
            line,
            wide_f32,
            jax.ShapeDtypeStruct((n, 2, piece, LANES), BF16),
        ],
        in_specs=[far] * 12,
        out_specs=[vmem] * 6,
        scratch_shapes=[
            pltpu.VMEM((positions, LANES), BF16),
            pltpu.VMEM((positions, LANES), BF16),
            pltpu.VMEM((positions, LANES), F32),
            pltpu.VMEM((4, positions, LANES), BF16),
            pltpu.VMEM((LANES, 4 * LANES), BF16),
            pltpu.VMEM((positions, LANES), BF16),
            pltpu.VMEM((2, 2 * rows, rows), BF16),
            pltpu.VMEM((2, rows, LANES), F32),
            pltpu.VMEM((2, 2 * LANES, 2 * LANES), BF16),
            pltpu.VMEM((2, 2 * LANES, 2 * LANES), BF16),
            pltpu.VMEM((2, rows, 2 * rows), BF16),
            pltpu.VMEM((1, LANES), F32),
            pltpu.VMEM((positions, LANES), F32),
            buffer(2),
            buffer(2),
            buffer(1),
            buffer(1),
            buffer(1),
            buffer(1),
            buffer(2),
            pltpu.VMEM((plane, share + 16, LANES), BF16),
            pltpu.VMEM((plane, share + 16, LANES), BF16),
            pltpu.VMEM((share + 8, LANES), F32),
            pltpu.VMEM((share + 8, LANES), F32),
            pltpu.VMEM((plane, share, LANES), F32),
            pltpu.VMEM((4, positions, LANES), BF16),
            pltpu.VMEM((4, LANES, LANES), BF16),
            pltpu.VMEM((positions, LANES), F32),
            pltpu.VMEM((rows, own * LANES), BF16),
            pltpu.VMEM((own * rows, 2 * LANES), BF16),
            pltpu.VMEM((own * rows, 2 * LANES), BF16),
            pltpu.VMEM((2 * rows, own * LANES), BF16),
            pltpu.VMEM((2 * rows, own * LANES), BF16),
            pltpu.VMEM((own * rows, 2 * LANES), F32),
            pltpu.VMEM((own * rows, 2 * LANES), F32),
            pltpu.VMEM((own * rows, 2 * LANES), F32),
            pltpu.SemaphoreType.DMA((12,)),
            pltpu.SemaphoreType.DMA((8,)),
            pltpu.SemaphoreType.DMA((8,)),
            pltpu.SemaphoreType.DMA((2, 2, CHUNKS)),
            pltpu.SemaphoreType.DMA((2, 2, CHUNKS)),
            pltpu.SemaphoreType.DMA((2, CHUNKS)),
            pltpu.SemaphoreType.DMA((2, CHUNKS)),
            pltpu.SemaphoreType.DMA((3,)),
            pltpu.SemaphoreType.DMA((3,)),
        ],
        compiler_params=pltpu.CompilerParams(
            collective_id=0, has_side_effects=True, vmem_limit_bytes=40 * 1024 * 1024
        ),
        name="hyena",
    )(*map(in_hbm, (keys, values, taps, cotangent, out_weight, queries, *tables(rows), gain)))
    outs = pl.pallas_call(
        functools.partial(finish, n),
        out_shape=[wide, wide, wide, wide, square, wide_f32, line],
        in_specs=[far] * 3 + [vmem] * 6,
        out_specs=[far] * 7,
        scratch_shapes=[
            pltpu.VMEM((positions, LANES), BF16),
            pltpu.VMEM((positions, LANES), BF16),
            pltpu.VMEM((1, LANES), F32),
            pltpu.VMEM((positions, LANES), F32),
            pltpu.VMEM((positions, LANES), BF16),
            pltpu.VMEM((positions, LANES), BF16),
            pltpu.VMEM((positions, LANES), F32),
            pltpu.SemaphoreType.DMA((10,)),
        ],
        compiler_params=pltpu.CompilerParams(vmem_limit_bytes=24 * 1024 * 1024),
        name="finish",
    )(*map(in_hbm, (keys, values, gain)), *first)
    return (*outs[:6], outs[6].reshape(LANES))


def solution(mesh):
    wide = P("seq", "chan")
    return jax.shard_map(
        functools.partial(local, mesh.shape["seq"]),
        mesh=mesh,
        in_specs=(wide, wide, wide, wide, P("chan", None), wide, P("chan")),
        out_specs=(wide, wide, wide, wide, P("chan", None), wide, P("chan")),
        check_vma=False,
    )
```

time: 74.4 us -> 50.4 us (0.68)
  local copies, waits for them, and re-layouts: 16.1 us -> 0 us
  Pallas kernels: 57.1 us -> 48.8 us
    unnamed x31 -> x0, local copies, waits for them, and re-layouts: 16.1 us -> none
    pallas_call x1 -> x2, Pallas kernels: 57.1 us -> 48.8 us  [the longest x1 46.3 us: local(): pl.pallas_call(functools.partial(kernel, n), out_shape=[wide, wide, squar...]
where the time goes in v2:
time: 50.4 us; the launch traced here: 49.4 us
  Pallas kernels  48.8 us (97%)
  between operations  0.64 us (1%)
    pallas_call x1, Pallas kernels, local(): pl.pallas_call(functools.partial(kernel, n), out_shape=[wide, wide, squar...  46.3 us
    pallas_call x1, Pallas kernels, local(): pl.pallas_call(functools.partial(finish, n), out_shape=[wide, wide, wide,...  2.48 us

profile of v2, /device:TPU:0, one launch (start us, length us, event | category | flops | bytes accessed | tf_op | source)
XLA Modules:
  0.0 49.4 jit_solution(17410537007274868339)
XLA Ops:
  0.6 46.3 %hyena.1 = (bf16[1024,128]{1,0:T(8,128)(2,1)S(1)}, bf16[1024,128]{1,0:T(8,128)(2,1)S(1)}, f32[128,512]{1,0:T(8,128)S(1)}, f32[1,128]{1,0:T(1,128)S(1)}, f32[1024...) custom-call(bf16[1024,128]{1,0:T(8,128)(2,1)} %keys_in.3, bf16[1024,128]{1,0:T(8,128)(2,1)} %values_in.3, ...), custom_call_target="tpu_custom_call" | custom-call | tf_op jit(solution)/shard_map/hyena/pallas_call | solution.py:591
  47.0 2.5 %finish.1 = (bf16[1024,128]{1,0:T(8,128)(2,1)}, bf16[1024,128]{1,0:T(8,128)(2,1)}, bf16[1024,128]{1,0:T(8,128)(2,1)}, bf16[1024,128]{1,0:T(8,128)(2,1)}, f32[128...) custom-call(bf16[1024,128]{1,0:T(8,128)(2,1)} %keys_in.3, bf16[1024,128]{1,0:T(8,128)(2,1)} %values_in.3, ...), custom_call_target="tpu_custom_call" | custom-call | tf_op jit(solution)/shard_map/finish/pallas_call | solution.py:655

commit v3 on v2

--- a/solution.py
+++ b/solution.py
@@ -14,6 +14,7 @@
 F32 = jnp.float32
 LANES = 128
 CHUNKS = 4
+RING = 4
 
 
 def split_table(table):
@@ -68,7 +69,10 @@
     gain_in,
     out_o,
     query_o,
+    key_o,
+    value_o,
     weight_o,
+    taps_o,
     skip_o,
     inner_cot,
     grad_recv,
@@ -100,6 +104,7 @@
     gated_all,
     columns,
     back,
+    mixed_all,
     xb,
     t_high,
     t_low,
@@ -168,6 +173,16 @@
     here, spot = me // plane, lax.rem(me, plane)
     across = 1 - here
 
+    depth = plane // RING
+    far_first = sorted(
+        ((dz, dx) for dz in range(depth) for dx in range(RING)),
+        key=lambda offset: -min(offset[0], depth - offset[0]) - min(offset[1], RING - offset[1]),
+    )
+
+    def place_at(offset):
+        dz, dx = offset
+        return lax.rem(spot // RING + dz, depth) * RING + lax.rem(spot + dx, RING)
+
     def send(src, dst, phase, peer):
         pltpu.make_async_remote_copy(
             src_ref=src,
@@ -182,12 +197,11 @@
         def at(ref, slot):
             return ref.at[slot] if index is None else ref.at[slot, index]
 
-        def step(offset, carry):
-            peer = half * plane + lax.rem(spot + offset, plane)
+        for offset in far_first:
+            if half is here and offset == (0, 0):
+                continue
+            peer = half * plane + place_at(offset)
             send(at(src, peer), at(dst, me), phase, peer)
-            return carry
-
-        lax.fori_loop(1 if half is here else 0, plane, step, 0)
         if half is here:
             if index is None:
                 dst[me] = src[me]
@@ -202,9 +216,15 @@
         part = buf.at[pl.ds(0, count)] if index is None else buf.at[pl.ds(0, count), index]
         pltpu.make_async_copy(part, part, sems.at[phase]).wait()
 
+    def turn(value, b):
+        stage[pl.ds(b, LANES, stride=blocks), :] = value.T
+
     def pack(value, dst, index):
         for b in range(blocks):
-            stage[pl.ds(b, LANES, stride=blocks), :] = value(b).T
+            turn(value(b), b)
+        put(dst, index)
+
+    def put(dst, index):
         dst[:, index] = stage[...].astype(BF16).reshape(n, piece, LANES)
 
     def unpack(src, index):
@@ -214,50 +234,37 @@
     def block(ref, b):
         return ref[b * LANES : (b + 1) * LANES, :].astype(F32)
 
-    def gather(src, buf, phase):
+    def gather_part(src, buf, phase, k):
         size = positions // CHUNKS
-        started = []
-        for k in range(CHUNKS):
-            part = pl.ds(k * size, size)
-            started.append(
-                pltpu.make_async_remote_copy(
-                    src_ref=src.at[part],
-                    dst_ref=buf.at[lane, part],
-                    send_sem=chan_send.at[phase, 0, k],
-                    recv_sem=chan_recv.at[phase, 0, k],
-                    device_id={"chan": mirror},
-                    device_id_type=MESH,
-                )
+        part = pl.ds(k * size, size)
+        started = [
+            pltpu.make_async_remote_copy(
+                src_ref=src.at[part],
+                dst_ref=buf.at[lane, part],
+                send_sem=chan_send.at[phase, way, k],
+                recv_sem=chan_recv.at[phase, way, k],
+                device_id={"chan": partner},
+                device_id_type=MESH,
             )
-            started[-1].start()
-        near = pltpu.make_async_remote_copy(
-            src_ref=src,
-            dst_ref=buf.at[lane],
-            send_sem=chan_send.at[phase, 1, 0],
-            recv_sem=chan_recv.at[phase, 1, 0],
+            for way, partner in enumerate((mirror, twin))
+        ]
+        for copy in started:
+            copy.start()
+        return started
+
+    def relay(buf, phase, started, k):
+        size = positions // CHUNKS
+        part = pl.ds(k * size, size)
+        started[k][0].wait_recv()
+        passed = pltpu.make_async_remote_copy(
+            src_ref=buf.at[mirror, part],
+            dst_ref=buf.at[mirror, part],
+            send_sem=relay_send.at[phase, k],
+            recv_sem=relay_recv.at[phase, k],
             device_id={"chan": twin},
             device_id_type=MESH,
         )
-        near.start()
-        return started, near
-
-    def relay(buf, phase, started):
-        size = positions // CHUNKS
-        passed = []
-        for k in range(CHUNKS):
-            part = pl.ds(k * size, size)
-            started[k].wait_recv()
-            passed.append(
-                pltpu.make_async_remote_copy(
-                    src_ref=buf.at[mirror, part],
-                    dst_ref=buf.at[mirror, part],
-                    send_sem=relay_send.at[phase, k],
-                    recv_sem=relay_recv.at[phase, k],
-                    device_id={"chan": twin},
-                    device_id_type=MESH,
-                )
-            )
-            passed[-1].start()
+        passed.start()
         return passed
 
     def forward(src, index, spec):
@@ -309,62 +316,93 @@
                 [y[:, :LANES].reshape(n, 8, LANES), y[:, LANES:].reshape(n, 8, LANES)], axis=1
             ).astype(BF16)
 
-    col_copies = [
-        pltpu.make_async_remote_copy(
-            src_ref=weight.at[:, pl.ds(pl.multiple_of(partner * LANES, LANES), LANES)],
-            dst_ref=columns.at[lane],
-            send_sem=col_send.at[k],
-            recv_sem=col_recv.at[k],
-            device_id={"chan": partner},
-            device_id_type=MESH,
+    team = min(8, plane)
+    first_spot, rank = spot // team * team, lax.rem(spot, team)
+    height = LANES // team
+    mine = pl.ds(pl.multiple_of(rank * height, height), height)
+    col_copies = []
+    for k, partner in enumerate((mirror, corner, twin)):
+        cols = pl.ds(pl.multiple_of(partner * LANES, LANES), LANES)
+        part = mine if k < 2 else pl.ds(0, LANES)
+        col_copies.append(
+            pltpu.make_async_remote_copy(
+                src_ref=weight.at[part, cols],
+                dst_ref=columns.at[lane, part],
+                send_sem=col_send.at[k],
+                recv_sem=col_recv.at[k],
+                device_id={"chan": partner},
+                device_id_type=MESH,
+            )
         )
-        for k, partner in enumerate((mirror, twin, corner))
-    ]
     share = 4 * LANES // plane
     count = LANES // share
     held = {}
 
-    def first_out():
-        exchange_all(first_send, first_recv, 0)
+    def inner_out():
+        exchange_all(first_send, first_recv, 0, 0)
+
+    def taps_out():
+        copies[2].wait()
+        pack(lambda b: block(taps, b), first_send, 1)
+        exchange_all(first_send, first_recv, 8, 1)
+
+    def signals_left():
+        await_all(first_send, send_sem, 0, index=0)
+        await_all(first_send, send_sem, 8, index=1)
 
     def cot_out():
-        held["cot"], held["cot_near"] = gather(cot_in, cot_all, 0)
-
-    def cot_relay():
-        for copy in copies[3:6]:
-            copy.wait()
-        held["cot_passed"] = relay(cot_all, 0, held["cot"])
+        held["cot"] = [gather_part(cot_in, cot_all, 0, k) for k in range(CHUNKS)]
 
     def columns_out():
+        copies[4].wait()
         for copy in col_copies:
             copy.start()
         columns[lane] = weight[:, pl.ds(pl.multiple_of(lane * LANES, LANES), LANES)]
 
+    def columns_on():
+        for k, origin in enumerate((mirror, corner)):
+            col_copies[k].wait_recv()
+            part = columns.at[origin, mine]
+            for step in range(1, team):
+                peer = here * plane + first_spot + lax.rem(rank + step, team)
+                send(part, part, 9 + k, peer)
+
     def cot_signal():
-        held["cot_near"].wait_recv()
-        for copy in held["cot_passed"]:
-            copy.wait_recv()
-        for b in range(blocks):
-            part = pl.ds(b * LANES, LANES)
-            total = jnp.zeros((LANES, LANES), F32)
-            for g in range(0, 4, 2):
-                left = jnp.concatenate([cot_all[g, part], cot_all[g + 1, part]], axis=1)
-                total += lax.dot_general(
-                    left,
-                    weight[:, g * LANES : (g + 2) * LANES],
-                    (((1,), (1,)), ((), ())),
-                    preferred_element_type=F32,
-                )
-            back[part, :] = total
-            inner_cot[part, :] = total * block(queries, b)
-        pack(lambda b: inner_cot[b * LANES : (b + 1) * LANES, :], cot_send, 0)
+        copies[3].wait()
+        copies[5].wait()
+        held["cot_passed"] = []
+        for k in range(CHUNKS + 1):
+            if k < CHUNKS:
+                held["cot_passed"].append(relay(cot_all, 0, held["cot"], k))
+            if k == 0:
+                continue
+            held["cot"][k - 1][1].wait_recv()
+            held["cot_passed"][k - 1].wait_recv()
+            size = blocks // CHUNKS
+            for b in range((k - 1) * size, k * size):
+                part = pl.ds(b * LANES, LANES)
+                total = jnp.zeros((LANES, LANES), F32)
+                for g in range(0, 4, 2):
+                    left = jnp.concatenate([cot_all[g, part], cot_all[g + 1, part]], axis=1)
+                    total += lax.dot_general(
+                        left,
+                        weight[:, g * LANES : (g + 2) * LANES],
+                        (((1,), (1,)), ((), ())),
+                        preferred_element_type=F32,
+                    )
+                back[part, :] = total
+                signal = total * block(queries, b)
+                inner_cot[part, :] = signal
+                turn(signal, b)
+        put(cot_send, 0)
         exchange_all(cot_send, cot_recv, 1)
 
     def conv_signal():
         for copy in copies[6:]:
             copy.wait()
-        await_all(first_recv, recv_sem, 0)
+        await_all(first_recv, recv_sem, 0, index=0)
         forward(first_recv, 0, spec_inner)
+        await_all(first_recv, recv_sem, 8, index=1)
         forward(first_recv, 1, spec_taps)
         inverse(spec_taps, spec_inner, False, conv_send, 0)
         exchange_all(conv_send, conv_recv, 2)
@@ -373,43 +411,53 @@
         await_all(cot_recv, recv_sem, 1)
         forward(cot_recv, 0, spec_cot)
         inverse(spec_taps, spec_cot, True, grad_send, 0)
+
+    def grad_out():
         exchange_all(grad_send, grad_recv, 3, 0)
 
     def taps_signal():
         inverse(spec_inner, spec_cot, True, grad_send, 1)
-        exchange_all(grad_send, grad_recv, 4, 1)
+        exchange(grad_send, grad_recv, 4, across, 1)
+
+    def taps_near():
+        exchange(grad_send, grad_recv, 4, here, 1)
 
     def gate():
         await_all(conv_recv, recv_sem, 2)
         conv = unpack(conv_recv, 0)
+        held["gated"] = []
+        for b in range(blocks):
+            part = pl.ds(b * LANES, LANES)
+            mixed = conv(b) + gain[...] * (block(keys, b) * block(values, b))
+            mixed_all[part, :] = mixed
+            gated_all[lane, part, :] = (block(queries, b) * mixed).astype(BF16)
+            if (b + 1) % (blocks // CHUNKS) == 0:
+                k = b // (blocks // CHUNKS)
+                held["gated"].append(gather_part(gated_all.at[lane], gated_all, 1, k))
         skip = jnp.zeros((8, LANES), F32)
         for b in range(blocks):
             part = pl.ds(b * LANES, LANES)
-            inner = block(keys, b) * block(values, b)
-            mixed = conv(b) + gain[...] * inner
-            gated_all[lane, part, :] = (block(queries, b) * mixed).astype(BF16)
-            query_o[part, :] = (back[part, :] * mixed).astype(BF16)
-            skip += jnp.sum((inner_cot[part, :] * inner).reshape(LANES // 8, 8, LANES), axis=0)
-        held["gated"], held["gated_near"] = gather(gated_all.at[lane], gated_all, 1)
+            product = inner_cot[part, :] * (block(keys, b) * block(values, b))
+            skip += jnp.sum(product.reshape(LANES // 8, 8, LANES), axis=0)
         held["skip"] = skip
+
+    def query_grads():
+        for b in range(blocks):
+            part = pl.ds(b * LANES, LANES)
+            query_o[part, :] = (back[part, :] * mixed_all[part, :]).astype(BF16)
 
     def weight_out():
         skip_high, skip_low = split(held["skip"])
         tail = jnp.concatenate([skip_high.astype(F32), skip_low.astype(F32)], axis=0).astype(BF16)
-        gated = gated_all[lane]
+        gated = gated_all[lane].T
         for g in range(4):
-            term = lax.dot_general(
-                gated, cot_all[g], (((0,), (0,)), ((), ())), preferred_element_type=F32
-            ).astype(BF16)
+            term = dot(gated, cot_all[g]).astype(BF16)
             weight_send[g * count : (g + 1) * count, :share, :] = term.reshape(count, share, LANES)
         weight_send[:, share:, :] = jnp.broadcast_to(tail[None], (plane, 16, LANES))
 
-        def spread(offset, carry):
-            place = lax.rem(spot + offset, plane)
+        for offset in far_first[:-1]:
+            place = place_at(offset)
             send(weight_send.at[place], weight_recv.at[spot], 5, here * plane + place)
-            return carry
-
-        lax.fori_loop(1, plane, spread, 0)
         weight_recv[spot] = weight_send[spot]
 
     def weight_pair():
@@ -421,24 +469,22 @@
 
     def weight_total():
         pltpu.make_async_copy(pair_recv, pair_recv, recv_sem.at[6]).wait()
-        sums = (pair_send[...] + pair_recv[...]) * scale
-        total_recv[spot] = sums[:share]
-        skip_o[...] = jnp.sum(sums[share:], axis=0, keepdims=True)
-
-        def collect(offset, carry):
-            place = lax.rem(spot + offset, plane)
-            send(total_recv.at[spot], total_recv.at[spot], 7, here * plane + place)
-            return carry
-
-        lax.fori_loop(1, plane, collect, 0)
+        sums = pair_send[...] + pair_recv[...]
+        total_recv[spot] = sums[:share].astype(BF16)
+        skip_o[...] = jnp.sum(sums[share:], axis=0, keepdims=True) * scale
+
+        for offset in far_first[:-1]:
+            send(total_recv.at[spot], total_recv.at[spot], 7, here * plane + place_at(offset))
 
     def gated_relay():
-        held["gated_passed"] = relay(gated_all, 1, held["gated"])
+        held["gated_passed"] = [relay(gated_all, 1, held["gated"], k) for k in range(CHUNKS)]
 
     def project():
-        held["gated_near"].wait_recv()
-        for copy in held["gated_passed"] + col_copies:
+        for copy in [pair[1] for pair in held["gated"]] + held["gated_passed"] + col_copies[2:]:
             copy.wait_recv()
+        others = columns.at[0, pl.ds(0, LANES - height)]
+        for phase in (9, 10):
+            pltpu.make_async_copy(others, others, recv_sem.at[phase]).wait()
         half = positions // 2
         for k in range(2):
             part = pl.ds(k * half, half)
@@ -448,15 +494,27 @@
                 total += dot(left, columns[g : g + 2].reshape(2 * LANES, LANES))
             out_o[part, :] = total.astype(BF16)
 
+    def factor_grads():
+        await_all(grad_recv, recv_sem, 3, index=0)
+        grad = unpack(grad_recv, 0)
+        for b in range(blocks):
+            part = pl.ds(b * LANES, LANES)
+            inner_grad = grad(b) + gain[...] * inner_cot[part, :]
+            key_o[part, :] = (inner_grad * block(values, b)).astype(BF16)
+            value_o[part, :] = (inner_grad * block(keys, b)).astype(BF16)
+
+    def taps_grads():
+        await_all(grad_recv, recv_sem, 4, index=1)
+        grad = unpack(grad_recv, 1)
+        for b in range(blocks):
+            taps_o[pl.ds(b * LANES, LANES), :] = grad(b) * scale
+
     def settle():
         await_all(total_recv, recv_sem, 7, plane - 1)
         for g in range(4):
-            weight_o[:, g * LANES : (g + 1) * LANES] = total_recv[
-                g * count : (g + 1) * count
-            ].reshape(LANES, LANES)
-        await_all(grad_recv, recv_sem, 3, index=0)
-        await_all(grad_recv, recv_sem, 4, index=1)
-        await_all(first_send, send_sem, 0)
+            weight_o[:, g * LANES : (g + 1) * LANES] = (
+                total_recv[g * count : (g + 1) * count].astype(F32).reshape(LANES, LANES) * scale
+            )
         await_all(cot_send, send_sem, 1)
         await_all(conv_send, send_sem, 2)
         await_all(grad_send, send_sem, 3, index=0)
@@ -464,108 +522,54 @@
         await_all(weight_send, send_sem, 5, plane - 1)
         pltpu.make_async_copy(pair_send, pair_send, send_sem.at[6]).wait()
         await_all(total_recv, send_sem, 7, plane - 1)
-        for name in ("cot", "cot_passed", "gated", "gated_passed"):
-            for copy in held[name]:
+        for name in ("cot", "gated"):
+            for copy in sum(held[name], held[name + "_passed"]):
                 copy.wait_send()
-        for copy in col_copies + [held["cot_near"], held["gated_near"]]:
+        others = columns.at[0, pl.ds(0, LANES - height)]
+        for phase in (9, 10):
+            pltpu.make_async_copy(others, others, send_sem.at[phase]).wait()
+        for copy in col_copies:
             copy.wait_send()
 
     copies[0].wait()
     copies[1].wait()
     pack(lambda b: block(keys, b) * block(values, b), first_send, 0)
-    copies[2].wait()
-    pack(lambda b: block(taps, b), first_send, 1)
     pl.semaphore_wait(barrier, n + 2)
     for step in (
-        first_out,
+        inner_out,
+        taps_out,
         cot_out,
         conv_signal,
-        cot_relay,
+        columns_out,
         cot_signal,
-        columns_out,
         gate,
         weight_out,
+        columns_on,
         grad_signal,
         weight_pair,
+        grad_out,
         taps_signal,
+        taps_near,
+        query_grads,
         weight_total,
         gated_relay,
+        signals_left,
         project,
+        factor_grads,
+        taps_grads,
         settle,
     ):
         step()
 
 
-def finish(
-    n,
-    keys_in,
-    values_in,
-    gain_in,
-    out_i,
-    query_i,
-    weight_i,
-    skip_i,
-    inner_cot,
-    grad_recv,
-    out_o,
-    query_o,
-    key_o,
-    value_o,
-    weight_o,
-    taps_o,
-    skip_o,
-    keys,
-    values,
-    gain,
-    stage,
-    key_v,
-    value_v,
-    taps_v,
-    sem,
-):
-    positions = keys.shape[0]
-    blocks = positions // LANES
-    scale = 1.0 / math.sqrt(positions * n)
-    loads = [
-        pltpu.make_async_copy(src, dst, sem.at[i])
-        for i, (src, dst) in enumerate(((keys_in, keys), (values_in, values), (gain_in, gain)))
+def store(*refs):
+    count = len(refs) // 2
+    copies = [
+        pltpu.make_async_copy(refs[i], refs[count + i], refs[-1].at[i]) for i in range(count)
     ]
-    stores = [
-        pltpu.make_async_copy(src, dst, sem.at[3 + i])
-        for i, (src, dst) in enumerate(
-            (
-                (out_i, out_o),
-                (query_i, query_o),
-                (weight_i, weight_o),
-                (skip_i, skip_o),
-                (taps_v, taps_o),
-                (key_v, key_o),
-                (value_v, value_o),
-            )
-        )
-    ]
-    for copy in loads + stores[:4]:
+    for copy in copies:
         copy.start()
-
-    def unpack(index):
-        stage[...] = grad_recv[:, index].astype(F32).reshape(positions, LANES)
-        return lambda b: stage[pl.ds(b, LANES, stride=blocks), :].T
-
-    grad = unpack(1)
-    for b in range(blocks):
-        taps_v[pl.ds(b * LANES, LANES), :] = grad(b) * scale
-    stores[4].start()
-    for copy in loads:
-        copy.wait()
-    grad = unpack(0)
-    for b in range(blocks):
-        part = pl.ds(b * LANES, LANES)
-        inner_grad = grad(b) + gain[...] * inner_cot[part, :]
-        key_v[part, :] = (inner_grad * values[part, :].astype(F32)).astype(BF16)
-        value_v[part, :] = (inner_grad * keys[part, :].astype(F32)).astype(BF16)
-    stores[5].start()
-    stores[6].start()
-    for copy in stores:
+    for copy in copies:
         copy.wait()
 
 
@@ -588,19 +592,15 @@
     def buffer(count):
         return pltpu.VMEM((n, count, piece, LANES), BF16)
 
-    first = pl.pallas_call(
+    shapes = [wide, wide, wide, wide, square, wide_f32, line]
+    results = pl.pallas_call(
         functools.partial(kernel, n),
-        out_shape=[
-            wide,
-            wide,
-            square,
-            line,
-            wide_f32,
-            jax.ShapeDtypeStruct((n, 2, piece, LANES), BF16),
-        ],
+        out_shape=shapes,
         in_specs=[far] * 12,
-        out_specs=[vmem] * 6,
+        out_specs=[vmem] * 7,
         scratch_shapes=[
+            pltpu.VMEM((positions, LANES), F32),
+            buffer(2),
             pltpu.VMEM((positions, LANES), BF16),
             pltpu.VMEM((positions, LANES), BF16),
             pltpu.VMEM((positions, LANES), F32),
@@ -625,9 +625,10 @@
             pltpu.VMEM((plane, share + 16, LANES), BF16),
             pltpu.VMEM((share + 8, LANES), F32),
             pltpu.VMEM((share + 8, LANES), F32),
-            pltpu.VMEM((plane, share, LANES), F32),
+            pltpu.VMEM((plane, share, LANES), BF16),
             pltpu.VMEM((4, positions, LANES), BF16),
             pltpu.VMEM((4, LANES, LANES), BF16),
+            pltpu.VMEM((positions, LANES), F32),
             pltpu.VMEM((positions, LANES), F32),
             pltpu.VMEM((rows, own * LANES), BF16),
             pltpu.VMEM((own * rows, 2 * LANES), BF16),
@@ -638,8 +639,8 @@
             pltpu.VMEM((own * rows, 2 * LANES), F32),
             pltpu.VMEM((own * rows, 2 * LANES), F32),
             pltpu.SemaphoreType.DMA((12,)),
-            pltpu.SemaphoreType.DMA((8,)),
-            pltpu.SemaphoreType.DMA((8,)),
+            pltpu.SemaphoreType.DMA((11,)),
+            pltpu.SemaphoreType.DMA((11,)),
             pltpu.SemaphoreType.DMA((2, 2, CHUNKS)),
             pltpu.SemaphoreType.DMA((2, 2, CHUNKS)),
             pltpu.SemaphoreType.DMA((2, CHUNKS)),
@@ -653,23 +654,14 @@
         name="hyena",
     )(*map(in_hbm, (keys, values, taps, cotangent, out_weight, queries, *tables(rows), gain)))
     outs = pl.pallas_call(
-        functools.partial(finish, n),
-        out_shape=[wide, wide, wide, wide, square, wide_f32, line],
-        in_specs=[far] * 3 + [vmem] * 6,
+        store,
+        out_shape=shapes,
+        in_specs=[vmem] * 7,
         out_specs=[far] * 7,
-        scratch_shapes=[
-            pltpu.VMEM((positions, LANES), BF16),
-            pltpu.VMEM((positions, LANES), BF16),
-            pltpu.VMEM((1, LANES), F32),
-            pltpu.VMEM((positions, LANES), F32),
-            pltpu.VMEM((positions, LANES), BF16),
-            pltpu.VMEM((positions, LANES), BF16),
-            pltpu.VMEM((positions, LANES), F32),
-            pltpu.SemaphoreType.DMA((10,)),
-        ],
-        compiler_params=pltpu.CompilerParams(vmem_limit_bytes=24 * 1024 * 1024),
-        name="finish",
-    )(*map(in_hbm, (keys, values, gain)), *first)
+        scratch_shapes=[pltpu.SemaphoreType.DMA((7,))],
+        compiler_params=pltpu.CompilerParams(vmem_limit_bytes=16 * 1024 * 1024),
+        name="store",
+    )(*results)
     return (*outs[:6], outs[6].reshape(LANES))
 
 

time: 50.4 us -> 48.1 us (0.954)
  Pallas kernels: 48.8 us -> 46.8 us
    pallas_call x2, Pallas kernels: 48.8 us -> 46.8 us  [the longest x1 45.5 us: local(): pl.pallas_call(functools.partial(kernel, n), out_shape=shapes, in_specs=[...]
where the time goes in v3:
time: 48.1 us; the launch traced here: 47.5 us
  Pallas kernels  46.8 us (97%)
  between operations  0.64 us (1%)
    pallas_call x1, Pallas kernels, local(): pl.pallas_call(functools.partial(kernel, n), out_shape=shapes, in_specs=[...  45.5 us
    pallas_call x1, Pallas kernels, local(): pl.pallas_call(store, out_shape=shapes, in_specs=[vmem] * 7, out_specs=[f...  1.29 us

profile of v3, /device:TPU:0, one launch (start us, length us, event | category | flops | bytes accessed | tf_op | source)
XLA Modules:
  0.0 47.5 jit_solution(2358803393721377994)
XLA Ops:
  0.6 45.5 %hyena.1 = (bf16[1024,128]{1,0:T(8,128)(2,1)S(1)}, bf16[1024,128]{1,0:T(8,128)(2,1)S(1)}, bf16[1024,128]{1,0:T(8,128)(2,1)S(1)}, bf16[1024,128]{1,0:T(8,128)(2,1...) custom-call(bf16[1024,128]{1,0:T(8,128)(2,1)} %keys_in.1, ...), custom_call_target="tpu_custom_call" | custom-call | tf_op jit(solution)/shard_map/hyena/pallas_call | solution.py:596
  46.2 1.3 %store.1 = (bf16[1024,128]{1,0:T(8,128)(2,1)}, bf16[1024,128]{1,0:T(8,128)(2,1)}, bf16[1024,128]{1,0:T(8,128)(2,1)}, bf16[1024,128]{1,0:T(8,128)(2,1)}, f32[128,...) custom-call(bf16[1024,128]{1,0:T(8,128)(2,1)S(1)} %get-tuple-element.21.refs_0_, ...), custom_call_target="tpu_custom_call" | custom-call | tf_op jit(solution)/shard_map/store/pallas_call | solution.py:656

commit v4 on v3

--- a/solution.py
+++ b/solution.py
@@ -137,18 +137,6 @@
     window = positions * n
     scale = 1.0 / math.sqrt(window)
 
-    barrier = pltpu.get_barrier_semaphore()
-
-    def greet(step, carry):
-        pl.semaphore_signal(
-            barrier, inc=1, device_id={"seq": lax.rem(me + step, n)}, device_id_type=MESH
-        )
-        return carry
-
-    for partner in (mirror, twin, corner):
-        pl.semaphore_signal(barrier, inc=1, device_id={"chan": partner}, device_id_type=MESH)
-    lax.fori_loop(1, n, greet, 0)
-
     pairs = (
         (keys_in, keys),
         (values_in, values),
@@ -166,9 +154,6 @@
     copies = [
         pltpu.make_async_copy(src, dst, table_sem.at[i]) for i, (src, dst) in enumerate(pairs)
     ]
-    for copy in copies:
-        copy.start()
-
     plane = n // 2
     here, spot = me // plane, lax.rem(me, plane)
     across = 1 - here
@@ -182,6 +167,20 @@
     def place_at(offset):
         dz, dx = offset
         return lax.rem(spot // RING + dz, depth) * RING + lax.rem(spot + dx, RING)
+
+    barrier = pltpu.get_barrier_semaphore()
+
+    def greet(place):
+        pl.semaphore_signal(barrier, inc=1, device_id=place, device_id_type=MESH)
+
+    for offset in far_first:
+        greet({"seq": across * plane + place_at(offset)})
+    for offset in far_first[:-1]:
+        greet({"seq": here * plane + place_at(offset)})
+    for partner in (mirror, corner, twin):
+        greet({"chan": partner})
+    for copy in copies:
+        copy.start()
 
     def send(src, dst, phase, peer):
         pltpu.make_async_remote_copy(
@@ -193,9 +192,9 @@
             device_id_type=MESH,
         ).start()
 
-    def exchange(src, dst, phase, half, index=None):
+    def exchange(src, dst, phase, half, index, part):
         def at(ref, slot):
-            return ref.at[slot] if index is None else ref.at[slot, index]
+            return ref.at[slot, index, part]
 
         for offset in far_first:
             if half is here and offset == (0, 0):
@@ -203,14 +202,11 @@
             peer = half * plane + place_at(offset)
             send(at(src, peer), at(dst, me), phase, peer)
         if half is here:
-            if index is None:
-                dst[me] = src[me]
-            else:
-                dst[me, index] = src[me, index]
-
-    def exchange_all(src, dst, phase, index=None):
-        exchange(src, dst, phase, across, index)
-        exchange(src, dst, phase, here, index)
+            dst[me, index, part] = src[me, index, part]
+
+    def exchange_all(src, dst, phase, index=0, part=slice(None)):
+        exchange(src, dst, phase, across, index, part)
+        exchange(src, dst, phase, here, index, part)
 
     def await_all(buf, sems, phase, count=n - 1, index=None):
         part = buf.at[pl.ds(0, count)] if index is None else buf.at[pl.ds(0, count), index]
@@ -267,14 +263,13 @@
         passed.start()
         return passed
 
-    def forward(src, index, spec):
-        for pair in range(own // 2):
+    def forward(src, index, spec, pairs):
+        for pair in pairs:
             x = src[:, index, 16 * pair : 16 * pair + 16, :].astype(F32)
             for half in range(2):
                 xb[:, (2 * pair + half) * LANES : (2 * pair + half + 1) * LANES] = (
                     x[:, 8 * half : 8 * half + 8, :].reshape(rows, LANES).astype(BF16)
                 )
-        for pair in range(own // 2):
             cols = xb[:, 2 * pair * LANES : (2 * pair + 2) * LANES]
             a = dot(fa[0], cols) + dot(fa[1], cols)
             for half in range(2):
@@ -285,36 +280,41 @@
                     [real * tw[0] - imag * tw[1], real * tw[1] + imag * tw[0]], axis=1
                 )
                 t_high[c * rows : (c + 1) * rows, :], t_low[c * rows : (c + 1) * rows, :] = split(t)
-        for c in range(own):
-            part = slice(c * rows, (c + 1) * rows)
-            spec[part, :] = (
-                dot(t_high[part, :], fb[0]) + dot(t_high[part, :], fb[1]) + dot(t_low[part, :], fb[0])
-            )
-
-    def inverse(left, right, conjugate, dst, index):
+            for c in (2 * pair, 2 * pair + 1):
+                part = slice(c * rows, (c + 1) * rows)
+                spec[part, :] = (
+                    dot(t_high[part, :], fb[0])
+                    + dot(t_high[part, :], fb[1])
+                    + dot(t_low[part, :], fb[0])
+                )
+
+    def inverse(left, right, conjugate, dst, index, pairs):
         sign = -1.0 if conjugate else 1.0
-        for c in range(own):
-            part = slice(c * rows, (c + 1) * rows)
-            l_real, l_imag = left[part, :LANES], sign * left[part, LANES:]
-            r_real, r_imag = right[part, :LANES], right[part, LANES:]
-            high, low = split(
-                jnp.concatenate(
-                    [l_real * r_real - l_imag * r_imag, l_real * r_imag + l_imag * r_real], axis=1
+        for pair in pairs:
+            for c in (2 * pair, 2 * pair + 1):
+                part = slice(c * rows, (c + 1) * rows)
+                l_real, l_imag = left[part, :LANES], sign * left[part, LANES:]
+                r_real, r_imag = right[part, :LANES], right[part, LANES:]
+                high, low = split(
+                    jnp.concatenate(
+                        [l_real * r_real - l_imag * r_imag, l_real * r_imag + l_imag * r_real],
+                        axis=1,
+                    )
                 )
-            )
-            y = dot(high, gb[0]) + dot(high, gb[1]) + dot(low, gb[0])
-            real, imag = y[:, :LANES], y[:, LANES:]
-            d_real = split(real * tw[0] + imag * tw[1])
-            d_imag = split(imag * tw[0] - real * tw[1])
-            cols = slice(c * LANES, (c + 1) * LANES)
-            d_high[:rows, cols], d_low[:rows, cols] = d_real
-            d_high[rows:, cols], d_low[rows:, cols] = d_imag
-        for pair in range(own // 2):
+                y = dot(high, gb[0]) + dot(high, gb[1]) + dot(low, gb[0])
+                real, imag = y[:, :LANES], y[:, LANES:]
+                d_real = split(real * tw[0] + imag * tw[1])
+                d_imag = split(imag * tw[0] - real * tw[1])
+                cols = slice(c * LANES, (c + 1) * LANES)
+                d_high[:rows, cols], d_low[:rows, cols] = d_real
+                d_high[rows:, cols], d_low[rows:, cols] = d_imag
             cols = slice(2 * pair * LANES, (2 * pair + 2) * LANES)
             y = dot(ga[0], d_high[:, cols]) + dot(ga[1], d_high[:, cols]) + dot(ga[0], d_low[:, cols])
             dst[:, index, 16 * pair : 16 * pair + 16, :] = jnp.concatenate(
                 [y[:, :LANES].reshape(n, 8, LANES), y[:, LANES:].reshape(n, 8, LANES)], axis=1
             ).astype(BF16)
+
+    every = range(own // 2)
 
     team = min(8, plane)
     first_spot, rank = spot // team * team, lax.rem(spot, team)
@@ -351,7 +351,10 @@
         await_all(first_send, send_sem, 8, index=1)
 
     def cot_out():
-        held["cot"] = [gather_part(cot_in, cot_all, 0, k) for k in range(CHUNKS)]
+        held["cot"] += [gather_part(cot_in, cot_all, 0, k) for k in range(1, CHUNKS)]
+
+    def cot_start():
+        held["cot"] = [gather_part(cot_in, cot_all, 0, 0)]
 
     def columns_out():
         copies[4].wait()
@@ -401,26 +404,26 @@
         for copy in copies[6:]:
             copy.wait()
         await_all(first_recv, recv_sem, 0, index=0)
-        forward(first_recv, 0, spec_inner)
+        forward(first_recv, 0, spec_inner, every)
         await_all(first_recv, recv_sem, 8, index=1)
-        forward(first_recv, 1, spec_taps)
-        inverse(spec_taps, spec_inner, False, conv_send, 0)
+        forward(first_recv, 1, spec_taps, every)
+        inverse(spec_taps, spec_inner, False, conv_send, 0, every)
         exchange_all(conv_send, conv_recv, 2)
 
-    def grad_signal():
+    def grad_pairs(pairs):
+        forward(cot_recv, 0, spec_cot, pairs)
+        inverse(spec_taps, spec_cot, True, grad_send, 0, pairs)
+
+    def grad_first():
         await_all(cot_recv, recv_sem, 1)
-        forward(cot_recv, 0, spec_cot)
-        inverse(spec_taps, spec_cot, True, grad_send, 0)
-
-    def grad_out():
+        grad_pairs(every)
+
+    def grad_rest():
         exchange_all(grad_send, grad_recv, 3, 0)
 
     def taps_signal():
-        inverse(spec_inner, spec_cot, True, grad_send, 1)
-        exchange(grad_send, grad_recv, 4, across, 1)
-
-    def taps_near():
-        exchange(grad_send, grad_recv, 4, here, 1)
+        inverse(spec_inner, spec_cot, True, grad_send, 1, every)
+        exchange_all(grad_send, grad_recv, 4, 1)
 
     def gate():
         await_all(conv_recv, recv_sem, 2)
@@ -536,6 +539,7 @@
     pack(lambda b: block(keys, b) * block(values, b), first_send, 0)
     pl.semaphore_wait(barrier, n + 2)
     for step in (
+        cot_start,
         inner_out,
         taps_out,
         cot_out,
@@ -545,11 +549,10 @@
         gate,
         weight_out,
         columns_on,
-        grad_signal,
+        grad_first,
         weight_pair,
-        grad_out,
+        grad_rest,
         taps_signal,
-        taps_near,
         query_grads,
         weight_total,
         gated_relay,

time: 48.1 us -> 46.1 us (0.958)
  Pallas kernels: 46.8 us -> 45.1 us
    pallas_call x1, Pallas kernels: 45.5 us -> 43.8 us  [local(): pl.pallas_call(functools.partial(kernel, n), out_shape=shapes, in_specs=[...]
where the time goes in v4:
time: 46.1 us; the launch traced here: 45.8 us
  Pallas kernels  45.1 us (98%)
  between operations  0.64 us (1%)
    pallas_call x1, Pallas kernels, local(): pl.pallas_call(functools.partial(kernel, n), out_shape=shapes, in_specs=[...  43.8 us
    pallas_call x1, Pallas kernels, local(): pl.pallas_call(store, out_shape=shapes, in_specs=[vmem] * 7, out_specs=[f...  1.29 us

profile of v4, /device:TPU:0, one launch (start us, length us, event | category | flops | bytes accessed | tf_op | source)
XLA Modules:
  0.0 45.8 jit_solution(5242339535521604150)
XLA Ops:
  0.6 43.8 %hyena.1 = (bf16[1024,128]{1,0:T(8,128)(2,1)S(1)}, bf16[1024,128]{1,0:T(8,128)(2,1)S(1)}, bf16[1024,128]{1,0:T(8,128)(2,1)S(1)}, bf16[1024,128]{1,0:T(8,128)(2,1...) custom-call(bf16[1024,128]{1,0:T(8,128)(2,1)} %keys_in.1, ...), custom_call_target="tpu_custom_call" | custom-call | tf_op jit(solution)/shard_map/hyena/pallas_call | solution.py:599
  44.5 1.3 %store.1 = (bf16[1024,128]{1,0:T(8,128)(2,1)}, bf16[1024,128]{1,0:T(8,128)(2,1)}, bf16[1024,128]{1,0:T(8,128)(2,1)}, bf16[1024,128]{1,0:T(8,128)(2,1)}, f32[128,...) custom-call(bf16[1024,128]{1,0:T(8,128)(2,1)S(1)} %get-tuple-element.21.refs_0_, ...), custom_call_target="tpu_custom_call" | custom-call | tf_op jit(solution)/shard_map/store/pallas_call | solution.py:659

commit v5 on v4

--- a/solution.py
+++ b/solution.py
@@ -72,10 +72,9 @@
     key_o,
     value_o,
     weight_o,
-    taps_o,
+    grad_recv,
     skip_o,
     inner_cot,
-    grad_recv,
     keys,
     values,
     taps,
@@ -410,19 +409,18 @@
         inverse(spec_taps, spec_inner, False, conv_send, 0, every)
         exchange_all(conv_send, conv_recv, 2)
 
-    def grad_pairs(pairs):
-        forward(cot_recv, 0, spec_cot, pairs)
-        inverse(spec_taps, spec_cot, True, grad_send, 0, pairs)
-
-    def grad_first():
+    def grad_signal():
         await_all(cot_recv, recv_sem, 1)
-        grad_pairs(every)
-
-    def grad_rest():
+        forward(cot_recv, 0, spec_cot, every)
+        inverse(spec_taps, spec_cot, True, grad_send, 0, every)
+
+    def grad_out():
         exchange_all(grad_send, grad_recv, 3, 0)
 
     def taps_signal():
         inverse(spec_inner, spec_cot, True, grad_send, 1, every)
+
+    def taps_grad_out():
         exchange_all(grad_send, grad_recv, 4, 1)
 
     def gate():
@@ -437,6 +435,8 @@
             if (b + 1) % (blocks // CHUNKS) == 0:
                 k = b // (blocks // CHUNKS)
                 held["gated"].append(gather_part(gated_all.at[lane], gated_all, 1, k))
+
+    def skip_sum():
         skip = jnp.zeros((8, LANES), F32)
         for b in range(blocks):
             part = pl.ds(b * LANES, LANES)
@@ -506,13 +506,8 @@
             key_o[part, :] = (inner_grad * block(values, b)).astype(BF16)
             value_o[part, :] = (inner_grad * block(keys, b)).astype(BF16)
 
-    def taps_grads():
+    def settle():
         await_all(grad_recv, recv_sem, 4, index=1)
-        grad = unpack(grad_recv, 1)
-        for b in range(blocks):
-            taps_o[pl.ds(b * LANES, LANES), :] = grad(b) * scale
-
-    def settle():
         await_all(total_recv, recv_sem, 7, plane - 1)
         for g in range(4):
             weight_o[:, g * LANES : (g + 1) * LANES] = (
@@ -546,32 +541,41 @@
         conv_signal,
         columns_out,
         cot_signal,
+        skip_sum,
         gate,
         weight_out,
         columns_on,
-        grad_first,
+        grad_signal,
         weight_pair,
-        grad_rest,
+        grad_out,
         taps_signal,
+        weight_total,
+        taps_grad_out,
         query_grads,
-        weight_total,
         gated_relay,
         signals_left,
         project,
         factor_grads,
-        taps_grads,
         settle,
     ):
         step()
 
 
-def store(*refs):
-    count = len(refs) // 2
+def store(scale, *refs):
+    sources, places, (stage, taps, sems) = list(refs[:7]), refs[7:14], refs[14:]
+    grad, sources[5] = sources[5], taps
     copies = [
-        pltpu.make_async_copy(refs[i], refs[count + i], refs[-1].at[i]) for i in range(count)
+        pltpu.make_async_copy(src, dst, sems.at[i])
+        for i, (src, dst) in enumerate(zip(sources, places))
     ]
-    for copy in copies:
+    for copy in copies[:5] + copies[6:]:
         copy.start()
+    positions = taps.shape[0]
+    blocks = positions // LANES
+    stage[...] = grad[:, 1].astype(F32).reshape(positions, LANES)
+    for b in range(blocks):
+        taps[pl.ds(b * LANES, LANES), :] = stage[pl.ds(b, LANES, stride=blocks), :].T * scale
+    copies[5].start()
     for copy in copies:
         copy.wait()
 
@@ -598,12 +602,11 @@
     shapes = [wide, wide, wide, wide, square, wide_f32, line]
     results = pl.pallas_call(
         functools.partial(kernel, n),
-        out_shape=shapes,
+        out_shape=[*shapes[:5], jax.ShapeDtypeStruct((n, 2, piece, LANES), BF16), line],
         in_specs=[far] * 12,
         out_specs=[vmem] * 7,
         scratch_shapes=[
             pltpu.VMEM((positions, LANES), F32),
-            buffer(2),
             pltpu.VMEM((positions, LANES), BF16),
             pltpu.VMEM((positions, LANES), BF16),
             pltpu.VMEM((positions, LANES), F32),
@@ -657,11 +660,15 @@
         name="hyena",
     )(*map(in_hbm, (keys, values, taps, cotangent, out_weight, queries, *tables(rows), gain)))
     outs = pl.pallas_call(
-        store,
+        functools.partial(store, 1.0 / math.sqrt(positions * n)),
         out_shape=shapes,
         in_specs=[vmem] * 7,
         out_specs=[far] * 7,
-        scratch_shapes=[pltpu.SemaphoreType.DMA((7,))],
+        scratch_shapes=[
+            pltpu.VMEM((positions, LANES), F32),
+            pltpu.VMEM((positions, LANES), F32),
+            pltpu.SemaphoreType.DMA((7,)),
+        ],
         compiler_params=pltpu.CompilerParams(vmem_limit_bytes=16 * 1024 * 1024),
         name="store",
     )(*results)

time: 46.1 us -> 45.8 us (level)
  no operation moved by 1% of the time
where the time goes in v5:
time: 45.8 us; the launch traced here: 45.7 us
  Pallas kernels  45 us (98%)
  between operations  0.64 us (1%)
    pallas_call x1, Pallas kernels, local(): pl.pallas_call(functools.partial(kernel, n), out_shape=[*shapes[:5], jax....  43.7 us
    pallas_call x1, Pallas kernels, local(): pl.pallas_call(functools.partial(store, 1.0 / math.sqrt(positions * n)),...  1.29 us

profile of v5, /device:TPU:0, one launch (start us, length us, event | category | flops | bytes accessed | tf_op | source)
XLA Modules:
  0.0 45.7 jit_solution(2144472004964284880)
XLA Ops:
  0.6 43.7 %hyena.1 = (bf16[1024,128]{1,0:T(8,128)(2,1)S(1)}, bf16[1024,128]{1,0:T(8,128)(2,1)S(1)}, bf16[1024,128]{1,0:T(8,128)(2,1)S(1)}, bf16[1024,128]{1,0:T(8,128)(2,1...) custom-call(bf16[1024,128]{1,0:T(8,128)(2,1)} %keys_in.1, ...), custom_call_target="tpu_custom_call" | custom-call | tf_op jit(solution)/shard_map/hyena/pallas_call | solution.py:603
  44.4 1.3 %store.1 = (bf16[1024,128]{1,0:T(8,128)(2,1)}, bf16[1024,128]{1,0:T(8,128)(2,1)}, bf16[1024,128]{1,0:T(8,128)(2,1)}, bf16[1024,128]{1,0:T(8,128)(2,1)}, f32[128,...) custom-call(bf16[1024,128]{1,0:T(8,128)(2,1)S(1)} %get-tuple-element.21.refs_0_, ...), custom_call_target="tpu_custom_call" | custom-call | tf_op jit(solution)/shard_map/store/pallas_call | solution.py:662

commit v6 on v5

--- a/solution.py
+++ b/solution.py
@@ -71,7 +71,7 @@
     query_o,
     key_o,
     value_o,
-    weight_o,
+    total_recv,
     grad_recv,
     skip_o,
     inner_cot,
@@ -95,11 +95,11 @@
     conv_send,
     conv_recv,
     grad_send,
+    skip_recv,
     weight_send,
     weight_recv,
     pair_send,
     pair_recv,
-    total_recv,
     gated_all,
     columns,
     back,
@@ -442,7 +442,10 @@
             part = pl.ds(b * LANES, LANES)
             product = inner_cot[part, :] * (block(keys, b) * block(values, b))
             skip += jnp.sum(product.reshape(LANES // 8, 8, LANES), axis=0)
-        held["skip"] = skip
+        high, low = split(skip)
+        skip_recv[spot] = jnp.concatenate([high.astype(F32), low.astype(F32)], axis=0).astype(BF16)
+        for offset in far_first[:-1]:
+            send(skip_recv.at[spot], skip_recv.at[spot], 11, here * plane + place_at(offset))
 
     def query_grads():
         for b in range(blocks):
@@ -450,13 +453,10 @@
             query_o[part, :] = (back[part, :] * mixed_all[part, :]).astype(BF16)
 
     def weight_out():
-        skip_high, skip_low = split(held["skip"])
-        tail = jnp.concatenate([skip_high.astype(F32), skip_low.astype(F32)], axis=0).astype(BF16)
         gated = gated_all[lane].T
         for g in range(4):
             term = dot(gated, cot_all[g]).astype(BF16)
-            weight_send[g * count : (g + 1) * count, :share, :] = term.reshape(count, share, LANES)
-        weight_send[:, share:, :] = jnp.broadcast_to(tail[None], (plane, 16, LANES))
+            weight_send[g * count : (g + 1) * count] = term.reshape(count, share, LANES)
 
         for offset in far_first[:-1]:
             place = place_at(offset)
@@ -465,9 +465,10 @@
 
     def weight_pair():
         await_all(weight_recv, recv_sem, 5, plane - 1)
-        sums = jnp.sum(weight_recv[...].astype(F32), axis=0)
-        pair_send[:share, :] = sums[:share]
-        pair_send[share:, :] = sums[share : share + 8] + sums[share + 8 :]
+        pair_send[:share, :] = jnp.sum(weight_recv[...].astype(F32), axis=0)
+        await_all(skip_recv, recv_sem, 11, plane - 1)
+        skip = jnp.sum(skip_recv[...].astype(F32), axis=0)
+        pair_send[share:, :] = skip[:8] + skip[8:]
         send(pair_send, pair_recv, 6, across * plane + spot)
 
     def weight_total():
@@ -509,15 +510,12 @@
     def settle():
         await_all(grad_recv, recv_sem, 4, index=1)
         await_all(total_recv, recv_sem, 7, plane - 1)
-        for g in range(4):
-            weight_o[:, g * LANES : (g + 1) * LANES] = (
-                total_recv[g * count : (g + 1) * count].astype(F32).reshape(LANES, LANES) * scale
-            )
         await_all(cot_send, send_sem, 1)
         await_all(conv_send, send_sem, 2)
         await_all(grad_send, send_sem, 3, index=0)
         await_all(grad_send, send_sem, 4, index=1)
         await_all(weight_send, send_sem, 5, plane - 1)
+        await_all(skip_recv, send_sem, 11, plane - 1)
         pltpu.make_async_copy(pair_send, pair_send, send_sem.at[6]).wait()
         await_all(total_recv, send_sem, 7, plane - 1)
         for name in ("cot", "gated"):
@@ -562,13 +560,13 @@
 
 
 def store(scale, *refs):
-    sources, places, (stage, taps, sems) = list(refs[:7]), refs[7:14], refs[14:]
-    grad, sources[5] = sources[5], taps
+    sources, places, (stage, weights, taps, sems) = list(refs[:7]), refs[7:14], refs[14:]
+    (total, grad), sources[4:6] = sources[4:6], (weights, taps)
     copies = [
         pltpu.make_async_copy(src, dst, sems.at[i])
         for i, (src, dst) in enumerate(zip(sources, places))
     ]
-    for copy in copies[:5] + copies[6:]:
+    for copy in copies[:4] + copies[6:]:
         copy.start()
     positions = taps.shape[0]
     blocks = positions // LANES
@@ -576,6 +574,12 @@
     for b in range(blocks):
         taps[pl.ds(b * LANES, LANES), :] = stage[pl.ds(b, LANES, stride=blocks), :].T * scale
     copies[5].start()
+    count = total.shape[0] // 4
+    for g in range(4):
+        weights[:, g * LANES : (g + 1) * LANES] = (
+            total[g * count : (g + 1) * count].astype(F32).reshape(LANES, LANES) * scale
+        )
+    copies[4].start()
     for copy in copies:
         copy.wait()
 
@@ -602,7 +606,12 @@
     shapes = [wide, wide, wide, wide, square, wide_f32, line]
     results = pl.pallas_call(
         functools.partial(kernel, n),
-        out_shape=[*shapes[:5], jax.ShapeDtypeStruct((n, 2, piece, LANES), BF16), line],
+        out_shape=[
+            *shapes[:4],
+            jax.ShapeDtypeStruct((plane, share, LANES), BF16),
+            jax.ShapeDtypeStruct((n, 2, piece, LANES), BF16),
+            line,
+        ],
         in_specs=[far] * 12,
         out_specs=[vmem] * 7,
         scratch_shapes=[
@@ -627,11 +636,11 @@
             buffer(1),
             buffer(1),
             buffer(2),
-            pltpu.VMEM((plane, share + 16, LANES), BF16),
-            pltpu.VMEM((plane, share + 16, LANES), BF16),
+            pltpu.VMEM((plane, 16, LANES), BF16),
+            pltpu.VMEM((plane, share, LANES), BF16),
+            pltpu.VMEM((plane, share, LANES), BF16),
             pltpu.VMEM((share + 8, LANES), F32),
             pltpu.VMEM((share + 8, LANES), F32),
-            pltpu.VMEM((plane, share, LANES), BF16),
             pltpu.VMEM((4, positions, LANES), BF16),
             pltpu.VMEM((4, LANES, LANES), BF16),
             pltpu.VMEM((positions, LANES), F32),
@@ -645,8 +654,8 @@
             pltpu.VMEM((own * rows, 2 * LANES), F32),
             pltpu.VMEM((own * rows, 2 * LANES), F32),
             pltpu.SemaphoreType.DMA((12,)),
-            pltpu.SemaphoreType.DMA((11,)),
-            pltpu.SemaphoreType.DMA((11,)),
+            pltpu.SemaphoreType.DMA((12,)),
+            pltpu.SemaphoreType.DMA((12,)),
             pltpu.SemaphoreType.DMA((2, 2, CHUNKS)),
             pltpu.SemaphoreType.DMA((2, 2, CHUNKS)),
             pltpu.SemaphoreType.DMA((2, CHUNKS)),
@@ -666,6 +675,7 @@
         out_specs=[far] * 7,
         scratch_shapes=[
             pltpu.VMEM((positions, LANES), F32),
+            pltpu.VMEM((LANES, 4 * LANES), F32),
             pltpu.VMEM((positions, LANES), F32),
             pltpu.SemaphoreType.DMA((7,)),
         ],

time: 45.8 us -> 45.8 us (level)
  no operation moved by 1% of the time
where the time goes in v6:
time: 45.8 us; the launch traced here: 45.7 us
  Pallas kernels  45 us (98%)
  between operations  0.64 us (1%)
    pallas_call x1, Pallas kernels, local(): pl.pallas_call(functools.partial(kernel, n), out_shape=[*shapes[:4], jax....  43.8 us
    pallas_call x1, Pallas kernels, local(): pl.pallas_call(functools.partial(store, 1.0 / math.sqrt(positions * n)),...  1.29 us

profile of v6, /device:TPU:0, one launch (start us, length us, event | category | flops | bytes accessed | tf_op | source)
XLA Modules:
  0.0 45.7 jit_solution(3538078605134669029)
XLA Ops:
  0.6 43.8 %hyena.1 = (bf16[1024,128]{1,0:T(8,128)(2,1)S(1)}, bf16[1024,128]{1,0:T(8,128)(2,1)S(1)}, bf16[1024,128]{1,0:T(8,128)(2,1)S(1)}, bf16[1024,128]{1,0:T(8,128)(2,1...) custom-call(bf16[1024,128]{1,0:T(8,128)(2,1)} %keys_in.1, ...), custom_call_target="tpu_custom_call" | custom-call | tf_op jit(solution)/shard_map/hyena/pallas_call | solution.py:607
  44.4 1.3 %store.1 = (bf16[1024,128]{1,0:T(8,128)(2,1)}, bf16[1024,128]{1,0:T(8,128)(2,1)}, bf16[1024,128]{1,0:T(8,128)(2,1)}, bf16[1024,128]{1,0:T(8,128)(2,1)}, f32[128,...) custom-call(bf16[1024,128]{1,0:T(8,128)(2,1)S(1)} %get-tuple-element.21.refs_0_, ...), custom_call_target="tpu_custom_call" | custom-call | tf_op jit(solution)/shard_map/store/pallas_call | solution.py:671

commit v7 on v6

--- a/solution.py
+++ b/solution.py
@@ -13,7 +13,7 @@
 BF16 = jnp.bfloat16
 F32 = jnp.float32
 LANES = 128
-CHUNKS = 4
+PARTS = ((2, 3, 3), (4, 4))
 RING = 4
 
 
@@ -230,8 +230,7 @@
         return ref[b * LANES : (b + 1) * LANES, :].astype(F32)
 
     def gather_part(src, buf, phase, k):
-        size = positions // CHUNKS
-        part = pl.ds(k * size, size)
+        part = pl.ds(sum(PARTS[phase][:k]) * LANES, PARTS[phase][k] * LANES)
         started = [
             pltpu.make_async_remote_copy(
                 src_ref=src.at[part],
@@ -248,8 +247,7 @@
         return started
 
     def relay(buf, phase, started, k):
-        size = positions // CHUNKS
-        part = pl.ds(k * size, size)
+        part = pl.ds(sum(PARTS[phase][:k]) * LANES, PARTS[phase][k] * LANES)
         started[k][0].wait_recv()
         passed = pltpu.make_async_remote_copy(
             src_ref=buf.at[mirror, part],
@@ -350,7 +348,7 @@
         await_all(first_send, send_sem, 8, index=1)
 
     def cot_out():
-        held["cot"] += [gather_part(cot_in, cot_all, 0, k) for k in range(1, CHUNKS)]
+        held["cot"] += [gather_part(cot_in, cot_all, 0, k) for k in range(1, len(PARTS[0]))]
 
     def cot_start():
         held["cot"] = [gather_part(cot_in, cot_all, 0, 0)]
@@ -373,15 +371,14 @@
         copies[3].wait()
         copies[5].wait()
         held["cot_passed"] = []
-        for k in range(CHUNKS + 1):
-            if k < CHUNKS:
+        for k in range(len(PARTS[0]) + 1):
+            if k < len(PARTS[0]):
                 held["cot_passed"].append(relay(cot_all, 0, held["cot"], k))
             if k == 0:
                 continue
             held["cot"][k - 1][1].wait_recv()
             held["cot_passed"][k - 1].wait_recv()
-            size = blocks // CHUNKS
-            for b in range((k - 1) * size, k * size):
+            for b in range(sum(PARTS[0][: k - 1]), sum(PARTS[0][:k])):
                 part = pl.ds(b * LANES, LANES)
                 total = jnp.zeros((LANES, LANES), F32)
                 for g in range(0, 4, 2):
@@ -432,8 +429,8 @@
             mixed = conv(b) + gain[...] * (block(keys, b) * block(values, b))
             mixed_all[part, :] = mixed
             gated_all[lane, part, :] = (block(queries, b) * mixed).astype(BF16)
-            if (b + 1) % (blocks // CHUNKS) == 0:
-                k = b // (blocks // CHUNKS)
+            k = len(held["gated"])
+            if b + 1 == sum(PARTS[1][: k + 1]):
                 held["gated"].append(gather_part(gated_all.at[lane], gated_all, 1, k))
 
     def skip_sum():
@@ -481,7 +478,9 @@
             send(total_recv.at[spot], total_recv.at[spot], 7, here * plane + place_at(offset))
 
     def gated_relay():
-        held["gated_passed"] = [relay(gated_all, 1, held["gated"], k) for k in range(CHUNKS)]
+        held["gated_passed"] = [
+            relay(gated_all, 1, held["gated"], k) for k in range(len(PARTS[1]))
+        ]
 
     def project():
         for copy in [pair[1] for pair in held["gated"]] + held["gated_passed"] + col_copies[2:]:
@@ -656,10 +655,10 @@
             pltpu.SemaphoreType.DMA((12,)),
             pltpu.SemaphoreType.DMA((12,)),
             pltpu.SemaphoreType.DMA((12,)),
-            pltpu.SemaphoreType.DMA((2, 2, CHUNKS)),
-            pltpu.SemaphoreType.DMA((2, 2, CHUNKS)),
-            pltpu.SemaphoreType.DMA((2, CHUNKS)),
-            pltpu.SemaphoreType.DMA((2, CHUNKS)),
+            pltpu.SemaphoreType.DMA((2, 2, max(map(len, PARTS)))),
+            pltpu.SemaphoreType.DMA((2, 2, max(map(len, PARTS)))),
+            pltpu.SemaphoreType.DMA((2, max(map(len, PARTS)))),
+            pltpu.SemaphoreType.DMA((2, max(map(len, PARTS)))),
             pltpu.SemaphoreType.DMA((3,)),
             pltpu.SemaphoreType.DMA((3,)),
         ],

time: 45.8 us -> 45.7 us (level)
  no operation moved by 1% of the time
where the time goes in v7:
time: 45.7 us; the launch traced here: 45.6 us
  Pallas kernels  45 us (98%)
  between operations  0.64 us (1%)
    pallas_call x1, Pallas kernels, local(): pl.pallas_call(functools.partial(kernel, n), out_shape=[*shapes[:4], jax....  43.7 us
    pallas_call x1, Pallas kernels, local(): pl.pallas_call(functools.partial(store, 1.0 / math.sqrt(positions * n)),...  1.29 us

profile of v7, /device:TPU:0, one launch (start us, length us, event | category | flops | bytes accessed | tf_op | source)
XLA Modules:
  0.0 45.6 jit_solution(18359007719809731736)
XLA Ops:
  0.6 43.7 %hyena.1 = (bf16[1024,128]{1,0:T(8,128)(2,1)S(1)}, bf16[1024,128]{1,0:T(8,128)(2,1)S(1)}, bf16[1024,128]{1,0:T(8,128)(2,1)S(1)}, bf16[1024,128]{1,0:T(8,128)(2,1...) custom-call(bf16[1024,128]{1,0:T(8,128)(2,1)} %keys_in.1, ...), custom_call_target="tpu_custom_call" | custom-call | tf_op jit(solution)/shard_map/hyena/pallas_call | solution.py:606
  44.3 1.3 %store.1 = (bf16[1024,128]{1,0:T(8,128)(2,1)}, bf16[1024,128]{1,0:T(8,128)(2,1)}, bf16[1024,128]{1,0:T(8,128)(2,1)}, bf16[1024,128]{1,0:T(8,128)(2,1)}, f32[128,...) custom-call(bf16[1024,128]{1,0:T(8,128)(2,1)S(1)} %get-tuple-element.21.refs_0_, ...), custom_call_target="tpu_custom_call" | custom-call | tf_op jit(solution)/shard_map/store/pallas_call | solution.py:670
